TPU v7x, 32 devices: a whole 2x2x4 slice. The times are simulated.
32 devices in a mesh: gx: 8 (over z, core), gy: 4 (over y, x).
Axes of the slice: x: 2, y: 2, z: 4, core: 2. Of those that a mesh axis runs over, the one named last changes fastest.
Arguments:
- atom_cell: int32 [3, 8, 8, 128, 576], P(None, 'gx', 'gy'), may hold values from 0 to 7
- atom_frac: float32 [3, 8, 8, 128, 576], P(None, 'gx', 'gy'), may hold values from 0 to 1
- atom_weight: float32 [8, 8, 128, 576], P('gx', 'gy'), may hold values from 0.5 to 1.5
- block_count: int32 [8, 8, 128], P('gx', 'gy'), may hold values from 384 to 576, as said below
- miller_h: int32 [8], replicated, may hold values from 9 to 12
- miller_k: int32 [8], replicated, may hold values from 9 to 12
- miller_l: int32 [8], replicated, may hold values from 9 to 204
Outputs:
- density: float32 [64, 64, 1024], P('gx', 'gy')
- intensity: float32 [128, 256], P(('gx', 'gy'))
Inputs may be any that keep to these rules, and one draw needn't show every extreme that they name: `block_count`: slots 0 to count - 1 of a block hold its atoms; every device holds a block with exactly 576 atoms.
All inputs are finite; a program needn't handle non-finite values.
Results may differ from a plain program's by a relative error of at most 0.0023.
Values sent between devices are 32-bit elements; how exact they have to be, the bound alone decides.
No kernel may reach another device: no remote copies, remote signals or barrier semaphores. Data moves between devices by JAX's collectives and lax.ppermute only.
A program may use at most 192 MiB of HBM per device.

v0:
```python
import math

import jax
import jax.numpy as jnp
from jax import lax
from jax.sharding import PartitionSpec as P

KERNEL_SIGMA = 0.9
NORMAL = 1.0 / (KERNEL_SIGMA * math.sqrt(2.0 * math.pi))
EXACT_DOT = lax.Precision.HIGHEST


def extended_2(cells, sides, width):
    for axis, dim in sides:
        count = lax.axis_size(axis)
        head = lax.slice_in_dim(cells, 0, width, axis=dim)
        tail = lax.slice_in_dim(cells, cells.shape[dim] - width, cells.shape[dim], axis=dim)
        cells = jnp.concatenate(
            [
                lax.ppermute(tail, axis, [(i, (i + 1) % count) for i in range(count)]),
                cells,
                lax.ppermute(head, axis, [((i + 1) % count, i) for i in range(count)]),
            ],
            axis=dim,
        )
    return cells


def kernel_taps(offsets, fraction):
    tap_rows = jnp.arange(16, dtype=jnp.int32)
    differ = tap_rows - offsets[..., None]
    inside = (differ >= 1) & (differ <= 8)
    distance = (differ - 4).astype(jnp.float32) - fraction[..., None]
    values = jnp.exp(distance * distance * (-0.5 / (KERNEL_SIGMA * KERNEL_SIGMA))) * NORMAL
    return jnp.where(inside, values, jnp.zeros_like(values))


def footprints(offsets, fraction, weights, counts):
    blocks, capacity = weights.shape
    slot_ids = jnp.arange(capacity, dtype=jnp.int32)
    occupied = (slot_ids[None, :] < counts[:, None]).astype(jnp.float32)
    taps_x = kernel_taps(offsets[0], fraction[0])
    taps_y = kernel_taps(offsets[1], fraction[1])
    taps_z = kernel_taps(offsets[2], fraction[2])
    scaled = ((weights * occupied)[..., None] * taps_z).astype(jnp.bfloat16)
    crossed = (
        (taps_x[..., :, None] * taps_y[..., None, :])
        .reshape(blocks, capacity, 256)
        .astype(jnp.bfloat16)
    )
    return jnp.einsum("bpc,bpm->bcm", scaled, crossed, preferred_element_type=jnp.float32)


def pad_along(values, along, leading, trailing):
    widths = [(0, 0)] * values.ndim
    widths[along] = (leading, trailing)
    return jnp.pad(values, widths)


def z_column(foot, depth_cells):
    nblocks = foot.shape[0]
    halves = foot.reshape(nblocks, 2, 8, 256)
    lower_half = pad_along(halves[:, 0], 0, 0, 1)
    upper_half = pad_along(halves[:, 1], 0, 1, 0)
    joined = (lower_half + upper_half).reshape((nblocks + 1) * 8, 256)
    interior = joined[4 : depth_cells + 4]
    folded = (
        interior
        + pad_along(joined[depth_cells + 4 :], 0, 0, depth_cells - 4)
        + pad_along(joined[:4], 0, depth_cells - 4, 0)
    )
    return jnp.transpose(folded, (1, 0))


def assemble(columns, blocks_x, blocks_y, depth_cells):
    pieces = columns.reshape(blocks_x, blocks_y, 2, 8, 2, 8, depth_cells)
    gathered = jnp.zeros((blocks_x + 1, blocks_y + 1, 8, 8, depth_cells), jnp.float32)
    for shift_x in range(2):
        for shift_y in range(2):
            moved = pad_along(pieces[:, :, shift_x, :, shift_y], 0, shift_x, 1 - shift_x)
            gathered = gathered + pad_along(moved, 1, shift_y, 1 - shift_y)
    gathered = jnp.transpose(gathered, (0, 2, 1, 3, 4))
    return gathered.reshape((blocks_x + 1) * 8, (blocks_y + 1) * 8, depth_cells)


def add_margins(extended, along, length):
    interior = lax.slice_in_dim(extended, 8, length + 8, axis=along)
    leading = lax.slice_in_dim(extended, 0, 4, axis=along)
    trailing = lax.slice_in_dim(extended, length + 12, length + 16, axis=along)
    return (
        interior
        + pad_along(leading, along, 0, length - 4)
        + pad_along(trailing, along, length - 4, 0)
    )


def phases(freqs, positions, extent):
    shifted = freqs[:, None] + jnp.arange(16, dtype=jnp.int32)[None, :] - 8
    product = positions[:, None, None] * shifted[None, :, :] % extent
    angles = product.astype(jnp.float32) * (2.0 * math.pi / extent)
    return (jnp.cos(angles), jnp.sin(angles))


def shards(atom_cell, atom_frac, atom_weight, block_count, miller_h, miller_k, miller_l):
    blocks_x, blocks_y, blocks_z, capacity = atom_weight.shape
    width_x = 8 * blocks_x
    width_y = 8 * blocks_y
    depth_cells = 8 * blocks_z
    columns_total = blocks_x * blocks_y
    offsets = atom_cell.reshape(3, columns_total, blocks_z, capacity)
    fraction = atom_frac.reshape(3, columns_total, blocks_z, capacity)
    weights = atom_weight.reshape(columns_total, blocks_z, capacity)
    counts = block_count.reshape(columns_total, blocks_z)

    def deposit(column_index):
        foot = footprints(
            lax.dynamic_index_in_dim(offsets, column_index, 1, False),
            lax.dynamic_index_in_dim(fraction, column_index, 1, False),
            lax.dynamic_index_in_dim(weights, column_index, 0, False),
            lax.dynamic_index_in_dim(counts, column_index, 0, False),
        )
        return z_column(foot, depth_cells)

    columns = lax.map(deposit, jnp.arange(columns_total, dtype=jnp.int32))
    padded = assemble(columns, blocks_x, blocks_y, depth_cells)
    extended = extended_2(padded, (("gx", 0),), 4)
    partway = add_margins(extended, 0, width_x)
    widened = extended_2(partway, (("gy", 1),), 4)
    density = add_margins(widened, 1, width_y)
    windows = miller_h.shape[0]
    index_x = lax.axis_index("gx")
    index_y = lax.axis_index("gy")
    total_x = width_x * lax.axis_size("gx")
    total_y = width_y * lax.axis_size("gy")
    cos_z, sin_z = phases(miller_l, jnp.arange(depth_cells, dtype=jnp.int32), depth_cells)
    table_z = jnp.concatenate([cos_z, -sin_z], axis=1).reshape(depth_cells, 2 * windows * 16)
    partial_value = jnp.dot(
        density.reshape(width_x * width_y, depth_cells),
        table_z,
        precision=EXACT_DOT,
        preferred_element_type=jnp.float32,
    )
    partial_value = partial_value.reshape(width_x, width_y, 2, windows, 16)
    part_real = partial_value[:, :, 0]
    part_imag = partial_value[:, :, 1]
    cell_y = index_y * width_y + jnp.arange(width_y, dtype=jnp.int32)
    cos_y, sin_y = phases(miller_k, cell_y, total_y)
    half_real = jnp.einsum("xywl,ywk->wxkl", part_real, cos_y, precision=EXACT_DOT) + jnp.einsum(
        "xywl,ywk->wxkl", part_imag, sin_y, precision=EXACT_DOT
    )
    half_imag = jnp.einsum("xywl,ywk->wxkl", part_imag, cos_y, precision=EXACT_DOT) - jnp.einsum(
        "xywl,ywk->wxkl", part_real, sin_y, precision=EXACT_DOT
    )
    half_real = half_real.reshape(windows, width_x, 256)
    half_imag = half_imag.reshape(windows, width_x, 256)
    cell_x = index_x * width_x + jnp.arange(width_x, dtype=jnp.int32)
    rows_here = windows * 16 // (lax.axis_size("gx") * lax.axis_size("gy"))
    row_ids = jnp.arange(rows_here * lax.axis_size(("gx", "gy")), dtype=jnp.int32)
    window_of = row_ids // 16
    shifted = jnp.take(miller_h, window_of, axis=0) + row_ids % 16 - 8
    product = shifted[:, None] * cell_x[None, :] % total_x
    angles = product.astype(jnp.float32) * (2.0 * math.pi / total_x)
    cos_x = jnp.cos(angles)
    sin_x = jnp.sin(angles)
    chosen_real = jnp.take(half_real, window_of, axis=0)
    chosen_imag = jnp.take(half_imag, window_of, axis=0)
    wave_real = jnp.einsum("rx,rxm->rm", cos_x, chosen_real, precision=EXACT_DOT) + jnp.einsum(
        "rx,rxm->rm", sin_x, chosen_imag, precision=EXACT_DOT
    )
    wave_imag = jnp.einsum("rx,rxm->rm", cos_x, chosen_imag, precision=EXACT_DOT) - jnp.einsum(
        "rx,rxm->rm", sin_x, chosen_real, precision=EXACT_DOT
    )
    summed = lax.psum_scatter(
        jnp.concatenate([wave_real, wave_imag], axis=1),
        ("gx", "gy"),
        scatter_dimension=0,
        tiled=True,
    )
    wave_real = summed[:, :256]
    wave_imag = summed[:, 256:]
    intensity = (wave_real * wave_real + wave_imag * wave_imag) / float(
        total_x * total_y * depth_cells
    )
    return (density, intensity)


def solution(mesh):
    in_specs = (
        P(None, "gx", "gy", None, None),
        P(None, "gx", "gy", None, None),
        P("gx", "gy", None, None),
        P("gx", "gy", None),
        P(),
        P(),
        P(),
    )
    out_specs = (P("gx", "gy", None), P(("gx", "gy"), None))
    return jax.shard_map(shards, mesh=mesh, in_specs=in_specs, out_specs=out_specs, check_vma=False)
```

profile of v0, /device:TPU:0, one launch (start us, length us, event | category | flops | bytes accessed | tf_op | source)
XLA Modules:
  0.0 391.9 jit_solution(13965032215901651026)
XLA Ops:
  7.2 2.9 copy.59
  10.1 2.8 copy.60
  13.0 0.2 copy.58
  13.2 206.0 %while.13 = (s32[]{:T(128)}, f32[2,256,1024]{2,1,0:T(8,128)}, s32[2]{0:T(128)S(1)}, s32[2,128]{1,0:T(2,128)S(1)}, f32[2,128,576]{2,1,0:T(8,128)S(1)}, /*index=5*...) while((s32[]{:T(128)}, f32[2,256,1024]{2,1,0:T(8,128)}, ...), condition=%wide.region_1.2_spmd, body=%wide.region_0.1_spmd.sunk | while | flops 683952128 | bytes 210700496 | solution.py:124
  13.2 0.6 dynamic_slice.49
  15.8 1.2 dynamic-slice_bitcast_fusion.9
  17.0 1.2 dynamic-slice_bitcast_fusion.8
  18.2 7.0 %multiply_select_fusion.5 = (f32[128,576,16]{1,2,0:T(8,128)}, f32[128,576,16]{1,2,0:T(8,128)}) fusion(f32[128,576]{1,0:T(8,128)S(1)} %get-tuple-element.222, s32[128,576]{1,0:T(8,128)S(1)} %get-tuple-element.223, f32[128,576]{1,0:T(8,128)S(1)} %get-tuple-element.224, s32[128,576]{1,0:T(8,128)S(1)} %get-tuple-element.225), kind=kLoop, calls=%fused_computation.3.clone.1 | loop fusion | flops 25952256 | bytes 10616832 | tf_op jit(solution)/shard_map/while/body/eval_jaxpr/jit(_where)/select_n | solution.py:35
  25.2 6.1 %copy.113 = f32[128,576,16]{0,2,1:T(8,128)} copy(f32[128,576,16]{1,2,0:T(8,128)} %get-tuple-element.226) | data formatting | bytes 9437184 | tf_op jit(solution)/shard_map/while/body/eval_jaxpr/jit(_where)/select_n | solution.py:35
  31.3 6.1 %copy.114 = f32[128,576,16]{0,2,1:T(8,128)} copy(f32[128,576,16]{1,2,0:T(8,128)} %get-tuple-element.227) | data formatting | bytes 9437184 | tf_op jit(solution)/shard_map/while/body/eval_jaxpr/jit(_where)/select_n | solution.py:35
  37.4 15.4 %multiply_convert_fusion.8 = bf16[128,576,16,16]{0,3,2,1:T(8,128)(2,1)} fusion(f32[128,576,16]{0,2,1:T(8,128)} %copy.113, f32[128,576,16]{0,2,1:T(8,128)} %copy.114), kind=kLoop, calls=%fused_computation.2.clone.1 | loop fusion | flops 37748736 | bytes 47185920 | tf_op jit(solution)/shard_map/while/body/eval_jaxpr/convert_element_type | solution.py:49
  52.8 46.4 %copy.115 = bf16[128,576,256]{2,1,0:T(8,128)(2,1)} copy(bf16[128,576,256]{0,2,1:T(8,128)(2,1)} %bitcast.156) | data formatting | bytes 75497472 | tf_op jit(solution)/shard_map/while/body/eval_jaxpr/convert_element_type | solution.py:49
  99.2 0.1 bitcast_select_fusion.3
  99.3 15.0 %fusion.126 = f32[128,2,8,256]{3,2,1,0:T(8,128)S(1)} fusion(bf16[128,576,256]{2,1,0:T(8,128)(2,1)} %copy.115, f32[128,576]{1,0:T(8,128)S(1)} %get-tuple-element.228, s32[128,576]{1,0:T(8,128)S(1)} %get-tuple-element.229, f32[128,576]{1,0:T(8,128)S(1)} %bitcast_select_fusion.3), kind=kOutput, calls=%fused_computation.28.clone.1 | convolution fusion | flops 619315200 | bytes 40730624 | tf_op jit(solution)/shard_map/while/body/eval_jaxpr/bpc,bpm->bcm/dot_general | solution.py:51
  114.4 0.2 slice_bitcast_fusion.9
  114.5 0.1 add_bitcast_fusion.2
  114.8 0.3 copy.116
  115.1 1.1 constant_dynamic-update-slice_fusion.2
  116.2 0.6 dynamic_slice.49
  118.7 1.2 dynamic-slice_bitcast_fusion.9
  120.0 1.2 dynamic-slice_bitcast_fusion.8
  121.2 7.0 %multiply_select_fusion.5 = (f32[128,576,16]{1,2,0:T(8,128)}, f32[128,576,16]{1,2,0:T(8,128)}) fusion(f32[128,576]{1,0:T(8,128)S(1)} %get-tuple-element.222, s32[128,576]{1,0:T(8,128)S(1)} %get-tuple-element.223, f32[128,576]{1,0:T(8,128)S(1)} %get-tuple-element.224, s32[128,576]{1,0:T(8,128)S(1)} %get-tuple-element.225), kind=kLoop, calls=%fused_computation.3.clone.1 | loop fusion | flops 25952256 | bytes 10616832 | tf_op jit(solution)/shard_map/while/body/eval_jaxpr/jit(_where)/select_n | solution.py:35
  128.2 6.1 %copy.113 = f32[128,576,16]{0,2,1:T(8,128)} copy(f32[128,576,16]{1,2,0:T(8,128)} %get-tuple-element.226) | data formatting | bytes 9437184 | tf_op jit(solution)/shard_map/while/body/eval_jaxpr/jit(_where)/select_n | solution.py:35
  134.3 6.1 %copy.114 = f32[128,576,16]{0,2,1:T(8,128)} copy(f32[128,576,16]{1,2,0:T(8,128)} %get-tuple-element.227) | data formatting | bytes 9437184 | tf_op jit(solution)/shard_map/while/body/eval_jaxpr/jit(_where)/select_n | solution.py:35
  140.4 15.4 %multiply_convert_fusion.8 = bf16[128,576,16,16]{0,3,2,1:T(8,128)(2,1)} fusion(f32[128,576,16]{0,2,1:T(8,128)} %copy.113, f32[128,576,16]{0,2,1:T(8,128)} %copy.114), kind=kLoop, calls=%fused_computation.2.clone.1 | loop fusion | flops 37748736 | bytes 47185920 | tf_op jit(solution)/shard_map/while/body/eval_jaxpr/convert_element_type | solution.py:49
  155.8 46.4 %copy.115 = bf16[128,576,256]{2,1,0:T(8,128)(2,1)} copy(bf16[128,576,256]{0,2,1:T(8,128)(2,1)} %bitcast.156) | data formatting | bytes 75497472 | tf_op jit(solution)/shard_map/while/body/eval_jaxpr/convert_element_type | solution.py:49
  202.3 15.0 %fusion.126 = f32[128,2,8,256]{3,2,1,0:T(8,128)S(1)} fusion(bf16[128,576,256]{2,1,0:T(8,128)(2,1)} %copy.115, f32[128,576]{1,0:T(8,128)S(1)} %get-tuple-element.228, s32[128,576]{1,0:T(8,128)S(1)} %get-tuple-element.229, f32[128,576]{1,0:T(8,128)S(1)} %bitcast_select_fusion.3), kind=kOutput, calls=%fused_computation.28.clone.1 | convolution fusion | flops 619315200 | bytes 40730624 | tf_op jit(solution)/shard_map/while/body/eval_jaxpr/bpc,bpm->bcm/dot_general | solution.py:51
  217.4 0.2 slice_bitcast_fusion.9
  217.5 0.1 add_bitcast_fusion.2
  217.8 0.3 copy.116
  218.1 1.1 constant_dynamic-update-slice_fusion.2
  219.2 1.7 slice_bitcast_fusion.7
  220.9 0.2 fusion.29
  221.1 0.2 copy.65
  221.3 0.5 collective-permute-start
  221.8 4.3 %collective-permute-start.1 = (f32[4,24,1024]{2,1,0:T(8,128)S(1)}, f32[4,24,1024]{2,1,0:T(8,128)S(1)}, u32[]{:S(2)}, u32[]{:S(2)}) collective-permute-start(f32[4,24,1024]{2,1,0:T(8,128)S(1)} %get-tuple-element.148), channel_id=1, source_target_pairs={{4,0},{8,4},{12,8},{16,12},{20,16},{24,20},{28,24},{0,28},{5,1},{9... | collective-permute-start | bytes 1179656 | tf_op jit(solution)/shard_map/ppermute | solution.py:22
  226.3 0.7 fusion.112
  227.0 5.2 %fusion.86 = s32[128]{0:T(128)S(1)} fusion(s32[]{:T(128)} %bitcast.29, s32[]{:T(128)} %bitcast.30, s32[]{:T(128)} %bitcast.31, s32[]{:T(128)} %bitcast.32, s32[]{:T(128)} %bitcast.33, s32[]{:T(128)} %bitcast.35, s32[]{:T(128)} %bitcast.34, s32[]{:T(128)} %bitcast.28), kind=kLoop, calls=%fused_computation.160 | loop fusion | flops 5888 | bytes 544 | tf_op jit(solution)/shard_map/sub | solution.py:160
  232.2 0.3 fusion.82
  232.5 2.1 fusion.64
  234.7 0.1 fusion.40
  234.9 1.8 collective-permute-start.2
  236.7 1.2 collective-permute-start.3
  237.8 0.1 pad_maximum_fusion
  237.9 4.2 %collective-permute-done.2 = f32[8,4,1024]{2,1,0:T(4,128)S(1)} collective-permute-done((f32[8,4,1024]{2,1,0:T(4,128)S(1)}, f32[8,4,1024]{2,1,0:T(4,128)S(1)}, u32[]{:S(2)}, u32[]{:S(2)}) %collective-permute-start.2) | collective-permute-done | bytes 131104 | tf_op jit(solution)/shard_map/ppermute | solution.py:20
  242.1 3.1 collective-permute-done.3
  245.3 0.1 fusion.44
  245.4 3.8 fusion.45
  249.2 0.1 slice_bitcast_fusion.2
  249.3 0.8 fusion.58
  250.2 0.8 fusion.62
  251.0 0.9 fusion.30
  251.9 0.2 reshape.271
  252.1 0.8 gather_fusion.1
  252.9 1.1 fusion.34
  254.0 1.1 fusion.32
  255.1 0.9 fusion.31
  256.0 0.2 reshape.270
  256.2 0.8 gather_fusion
  257.0 1.1 fusion.38
  258.1 1.1 fusion.36
  259.3 0.7 pad_maximum_fusion.1
  260.0 123.6 %all-reduce.19.cloned.1.call-done = f32[128,512]{1,0:T(8,128)} async-done(((f32[128,512]{1,0:T(8,128)}), f32[128,512]{1,0:T(8,128)}) %all-reduce.19.cloned.1.call-update) | async-done | bytes 262160
  383.6 1.4 fusion.84
  (35 shorter events, 0.7 us)
Async XLA Ops:
  7.2 5.8 %copy-start = (f32[1,2,128,576]{2,3,1,0:T(8,128)S(1)}, f32[1,2,128,576]{2,3,1,0:T(8,128)}, u32[]{:S(2)}) copy-start(f32[1,2,128,576]{2,3,1,0:T(8,128)} %param.13) | copy-start | bytes 1769476
  7.2 6.0 %copy-start.5 = (s32[1,2,128]{2,1,0:T(2,128)S(1)}, s32[1,2,128]{2,1,0:T(2,128)}, u32[]{:S(2)}) copy-start(s32[1,2,128]{2,1,0:T(2,128)} %param.14) | copy-start | bytes 3076
  7.2 376.4 %all-reduce.19.cloned.1.call-start = ((), (), s32[]{:S(2)}) async-start(), calls=%async_computation | async-start | bytes 524288
  220.8 5.3 %copy-start.3 = (s32[8]{0:T(128)S(1)}, s32[8]{0:T(128)}, u32[]{:S(2)}) copy-start(s32[8]{0:T(128)} %param.17) | copy-start | bytes 100
  220.8 5.4 %copy-start.4 = (s32[8]{0:T(128)S(1)}, s32[8]{0:T(128)}, u32[]{:S(2)}) copy-start(s32[8]{0:T(128)} %param.16) | copy-start | bytes 100
  220.8 5.4 %copy-start.2 = (s32[8]{0:T(128)S(1)}, s32[8]{0:T(128)}, u32[]{:S(2)}) copy-start(s32[8]{0:T(128)} %param.15) | copy-start | bytes 100
  221.3 13.3 %collective-permute-start = (f32[4,24,1024]{2,1,0:T(8,128)S(1)}, f32[4,24,1024]{2,1,0:T(8,128)S(1)}, u32[]{:S(2)}, u32[]{:S(2)}) collective-permute-start(f32[4,24,1024]{2,1,0:T(8,128)S(1)} %get-tuple-element.147), channel_id=1, source_target_pairs={{0,4},{4,8},{8,12},{12,16},{16,20},{20,24},{24,28},{28,0},{1,5},{5... | collective-permute-start | bytes 1179656 | tf_op jit(solution)/shard_map/ppermute | solution.py:20
  221.8 12.8 %collective-permute-start.1 = (f32[4,24,1024]{2,1,0:T(8,128)S(1)}, f32[4,24,1024]{2,1,0:T(8,128)S(1)}, u32[]{:S(2)}, u32[]{:S(2)}) collective-permute-start(f32[4,24,1024]{2,1,0:T(8,128)S(1)} %get-tuple-element.148), channel_id=1, source_target_pairs={{4,0},{8,4},{12,8},{16,12},{20,16},{24,20},{28,24},{0,28},{5,1},{9... | collective-permute-start | bytes 1179656 | tf_op jit(solution)/shard_map/ppermute | solution.py:22
  234.9 7.3 %collective-permute-start.2 = (f32[8,4,1024]{2,1,0:T(4,128)S(1)}, f32[8,4,1024]{2,1,0:T(4,128)S(1)}, u32[]{:S(2)}, u32[]{:S(2)}) collective-permute-start(f32[8,4,1024]{2,1,0:T(4,128)S(1)} %get-tuple-element.151), channel_id=1, source_target_pairs={{0,1},{1,2},{2,3},{3,0},{4,5},{5,6},{6,7},{7,4},{8,9},{9,10},{10,1... | collective-permute-start | bytes 393224 | tf_op jit(solution)/shard_map/ppermute | solution.py:20
  236.7 8.6 %collective-permute-start.3 = (f32[8,4,1024]{2,1,0:T(4,128)S(1)}, f32[8,4,1024]{2,1,0:T(4,128)S(1)}, u32[]{:S(2)}, u32[]{:S(2)}) collective-permute-start(f32[8,4,1024]{2,1,0:T(4,128)S(1)} %get-tuple-element.152), channel_id=1, source_target_pairs={{1,0},{2,1},{3,2},{0,3},{5,4},{6,5},{7,6},{4,7},{9,8},{10,9},{11,1... | collective-permute-start | bytes 393224 | tf_op jit(solution)/shard_map/ppermute | solution.py:22
  245.4 7.5 %copy-start.1 = (f32[8,16,1024]{2,1,0:T(8,128)}, f32[8,16,1024]{2,1,0:T(8,128)S(1)}, u32[]{:S(2)}) copy-start(f32[8,16,1024]{2,1,0:T(8,128)S(1)} %fusion.44) | copy-start | bytes 1572868
Sparse Core Ops, SparseCore 0:
  260.2 123.4 all-reduce.18
where the time goes:
time: 395 us; the launch traced here: 392 us
  local copies, waits for them, and re-layouts  137 us (35%)
  waiting for transfers between devices  131 us (33%)
  other arithmetic  55.8 us (14%)
  matrix products  41.7 us (11%)
  between operations  14.3 us (4%)
  starting transfers between devices  7.8 us (2%)
  loops' own time  4.02 us (1%)
    unnamed x2, waiting for transfers between devices  124 us
    convert_element_type x2, local copies, waits for them, and re-layouts, footprints(): crossed = (taps_x[..., :, None] * taps_y[..., None, :]).reshape(blocks, c...  92.8 us
    convert_element_type x2, other arithmetic, footprints(): crossed = (taps_x[..., :, None] * taps_y[..., None, :]).reshape(blocks, c...  30.8 us
    dot_general x2, matrix products, footprints(): jnp.einsum('bpc,bpm->bcm', scaled, crossed, preferred_element_type=jnp.fl...  30 us
    select_n x4, local copies, waits for them, and re-layouts, kernel_taps(): return jnp.where(inside, values, jnp.zeros_like(values))  24.4 us
    select_n x2, other arithmetic, kernel_taps(): return jnp.where(inside, values, jnp.zeros_like(values))  13.9 us
  transfers between devices with their start and end apart: 5, of which 3 were waited for; matrix products, arithmetic and copies ran while one was open for 2% of the time, Pallas kernels for 0%

commit v1 on v0

v1 whole, which is shorter than its diff:
```python
import functools
import math
import jax, jax.numpy as jnp
from jax import lax
from jax.experimental import pallas as pl
from jax.experimental.pallas import tpu as pltpu
from jax.sharding import PartitionSpec as P
KERNEL_SIGMA=0.9
NORMAL=1.0/(KERNEL_SIGMA*math.sqrt(2.0*math.pi))
NT=(((1,),(1,)),((),()))
SCALE=math.sqrt(0.5/math.log(2.0))/KERNEL_SIGMA
LOGN=math.log2(NORMAL)

def deposit_body(count_ref,cell_ref,frac_ref,weight_ref,grid_ref,rows_ref,tx_ref,cross_ref,line_ref,*,blocks_z,cap):
    column=pl.program_id(0); chunk=pl.program_id(1)
    depth=8*blocks_z
    @pl.when(chunk==0)
    def _():
        line_ref[...]=jnp.zeros_like(line_ref)
    two=2*cap
    def paired(v): return jnp.concatenate([v[0:8],v[8:16]],axis=1)
    for d in range(3):
        cell=cell_ref[d,0,0].astype(jnp.float32)
        rows_ref[2*d]=paired(cell)
        rows_ref[2*d+1]=paired((cell+frac_ref[d,0,0])*SCALE)
    row16=lax.broadcasted_iota(jnp.int32,(16,cap),0)
    counts=jnp.zeros((16,cap),jnp.int32)
    for r in range(16):
        counts=jnp.where(row16==r,count_ref[0,column,chunk*16+r],counts)
    slots=lax.broadcasted_iota(jnp.int32,(16,cap),1)
    rows_ref[6]=paired(jnp.where(slots<counts,weight_ref[0,0],0.0))
    r8=lax.broadcasted_iota(jnp.int32,(8,two),0).astype(jnp.float32)
    low=(r8-4.0)*SCALE; high=(r8+4.0)*SCALE
    def taps(d,i):
        inside=r8>rows_ref[2*d,i:i+1,:]
        dist=jnp.where(inside,low,high)-rows_ref[2*d+1,i:i+1,:]
        val=jnp.exp2(LOGN-dist*dist)
        return inside,val
    edge=cap//128*128
    lanes=lax.broadcasted_iota(jnp.int32,(16,128),1)+edge
    for i in range(8):
        slot=i%2
        mx,vx=taps(0,i);
        tx_ref[slot,0:8]=jnp.where(mx,vx,0.0); tx_ref[slot,8:16]=jnp.where(mx,0.0,vx)
        my,vy=taps(1,i)
        ty=jnp.concatenate([jnp.where(my,vy,0.0),jnp.where(my,0.0,vy)],axis=0)
        mz,vz=taps(2,i); vz=vz*rows_ref[6,i:i+1,:]
        z=jnp.concatenate([jnp.where(mz,vz,0.0),jnp.where(mz,0.0,vz)],axis=0)
        for a in range(16):
            cross_ref[slot,16*a:16*a+16,:]=(tx_ref[slot,a:a+1,:]*ty).astype(jnp.bfloat16)
        if cap%128:
            mid=z[:,edge:edge+128]
            nz=jnp.zeros((16,edge),jnp.float32)
            za=jnp.concatenate([z[:,:edge],jnp.where(lanes<cap,mid,0.0),nz],axis=1)
            zb=jnp.concatenate([nz,jnp.where(lanes<cap,0.0,mid),z[:,edge+128:]],axis=1)
        else:
            nz=jnp.zeros((16,cap),jnp.float32)
            za=jnp.concatenate([z[:,:cap],nz],axis=1); zb=jnp.concatenate([nz,z[:,cap:]],axis=1)
        lhs=jnp.concatenate([za,zb],axis=0).astype(jnp.bfloat16)
        out=lax.dot_general(lhs,cross_ref[slot],NT,preferred_element_type=jnp.float32)
        base=pl.multiple_of(chunk*128+8*i,8)
        line_ref[pl.ds(base,16),:]+=out[0:16]
        line_ref[pl.ds(base+64,16),:]+=out[16:32]
    @pl.when(chunk==pl.num_programs(1)-1)
    def _():
        line_ref[4:8,:]+=line_ref[depth+4:depth+8,:]
        line_ref[depth:depth+4,:]+=line_ref[0:4,:]
        for c in range(depth//128):
            part=jnp.transpose(line_ref[128*c+4:128*c+132,:]).reshape(16,16,128)
            @pl.when(column==0)
            def _():
                grid_ref[:,0:16,128*c:128*c+128]=part
                grid_ref[:,16:24,128*c:128*c+128]=jnp.zeros((16,8,128),jnp.float32)
            @pl.when(column==1)
            def _():
                grid_ref[:,8:24,128*c:128*c+128]+=part

def deposit(cell,frac,weight,count):
    _,bx,by,bz,cap=cell.shape
    body=functools.partial(deposit_body,blocks_z=bz,cap=cap)
    return pl.pallas_call(body,
        grid=(by,bz//16),
        in_specs=[pl.BlockSpec(memory_space=pltpu.SMEM),
                  pl.BlockSpec((3,1,1,16,cap),lambda j,c:(0,0,j,c,0)),
                  pl.BlockSpec((3,1,1,16,cap),lambda j,c:(0,0,j,c,0)),
                  pl.BlockSpec((1,1,16,cap),lambda j,c:(0,j,c,0))],
        out_specs=pl.BlockSpec((16,8*by+8,8*bz),lambda j,c:(0,0,0)),
        out_shape=jax.ShapeDtypeStruct((16,8*by+8,8*bz),jnp.float32),
        scratch_shapes=[pltpu.VMEM((7,8,2*cap),jnp.float32),pltpu.VMEM((2,16,2*cap),jnp.float32),
                        pltpu.VMEM((2,256,2*cap),jnp.bfloat16),pltpu.VMEM((8*bz+8,256),jnp.float32)],
        compiler_params=pltpu.CompilerParams(vmem_limit_bytes=40<<20),
    )(count,cell,frac,weight)


def turn(freqs, place, extent):
    product = freqs * place
    if extent & (extent - 1) == 0:
        product = product & (extent - 1)
    else:
        product = lax.rem(lax.rem(product, extent) + extent, extent)
    angle = product.astype(jnp.float32) * (2.0 * math.pi / extent)
    return jnp.cos(angle), jnp.sin(angle)


def times(one, other):
    return (
        one[0] * other[0] - one[1] * other[1],
        one[0] * other[1] + one[1] * other[0],
    )


def split(value):
    head = value.astype(jnp.bfloat16)
    return head, (value - head.astype(jnp.float32)).astype(jnp.bfloat16)


def amplitude_body(
    place_ref, h_ref, k_ref, l_ref, grid_ref, out_ref,
    phase_ref, shift_ref, along_z_ref, half_ref, wave_ref, *, total_x, total_y
):
    rows_x, rows_y, depth = grid_ref.shape
    windows = h_ref.shape[0]
    wide = 16 * windows

    def centres(ref, shape):
        window = lax.broadcasted_iota(jnp.int32, shape, 1) // 16
        found = jnp.zeros(shape, jnp.int32)
        for w in range(windows):
            found = jnp.where(window == w, ref[w], found)
        return found

    block = 32
    below = lax.broadcasted_iota(jnp.int32, (block, wide), 0)
    freq_l = centres(l_ref, (block, wide)) + lax.rem(lax.broadcasted_iota(jnp.int32, (block, wide), 1), 16) - 8
    fine = turn(freq_l, below, depth)
    coarse = turn(freq_l, below * block, depth)
    shift_ref[0] = coarse[0]
    shift_ref[1] = coarse[1]
    for step in range(depth // block):
        now = times(fine, (shift_ref[0, step : step + 1], shift_ref[1, step : step + 1]))
        at = pl.ds(step * block, block)
        phase_ref[at, 0:wide] = now[0]
        phase_ref[at, wide : 2 * wide] = -now[1]
    value, rest = split(grid_ref[...].reshape(rows_x * rows_y, depth))
    table, left = split(phase_ref[...])

    def dot(a, b):
        return jnp.dot(a, b, preferred_element_type=jnp.float32)

    along_z_ref[...] = (dot(value, table) + (dot(value, left) + dot(rest, table))).reshape(
        rows_x, rows_y, 2 * wide
    )
    row16 = lax.broadcasted_iota(jnp.int32, (16, wide), 0)
    freq_k = centres(k_ref, (16, wide)) + row16 - 8
    now = turn(freq_k, place_ref[1] + 2 * total_y, total_y)
    step = turn(freq_k, 1, total_y)
    for y in range(rows_y):
        phase_ref[pl.ds(32 * y, 16), 0:wide] = now[0]
        phase_ref[pl.ds(32 * y + 16, 16), 0:wide] = now[1]
        now = times(now, step)
    group = 4
    for x in range(0, rows_x, group):
        real = [jnp.zeros((16, wide), jnp.float32)] * group
        imag = [jnp.zeros((16, wide), jnp.float32)] * group
        for y in range(rows_y):
            cos = phase_ref[pl.ds(32 * y, 16), 0:wide]
            sin = phase_ref[pl.ds(32 * y + 16, 16), 0:wide]
            for g in range(group):
                a = along_z_ref[x + g, y : y + 1, 0:wide]
                b = along_z_ref[x + g, y : y + 1, wide : 2 * wide]
                real[g] = real[g] + (a * cos + b * sin)
                imag[g] = imag[g] + (b * cos - a * sin)
        for g in range(group):
            half_ref[x + g, 0:16] = real[g]
            half_ref[x + g, 16:32] = imag[g]
    freq_h = centres(h_ref, (16, wide)) + row16 - 8
    now = turn(freq_h, place_ref[0] + 2 * total_x, total_x)
    step = turn(freq_h, 1, total_x)
    for x in range(rows_x):
        phase_ref[pl.ds(32 * x, 16), wide : 2 * wide] = now[0]
        phase_ref[pl.ds(32 * x + 16, 16), wide : 2 * wide] = now[1]
        now = times(now, step)
    for h in range(0, 16, group):
        real = [jnp.zeros((16, wide), jnp.float32)] * group
        imag = [jnp.zeros((16, wide), jnp.float32)] * group
        for x in range(rows_x):
            a = half_ref[x, 0:16]
            b = half_ref[x, 16:32]
            for g in range(group):
                cos = phase_ref[32 * x + h + g : 32 * x + h + g + 1, wide : 2 * wide]
                sin = phase_ref[32 * x + 16 + h + g : 32 * x + 17 + h + g, wide : 2 * wide]
                real[g] = real[g] + (a * cos + b * sin)
                imag[g] = imag[g] + (b * cos - a * sin)
        for g in range(group):
            wave_ref[pl.ds(32 * (h + g), 16)] = real[g]
            wave_ref[pl.ds(32 * (h + g) + 16, 16)] = imag[g]
    turned = jnp.transpose(wave_ref[...])
    pieces, _, lanes = out_ref.shape
    per_window = pieces // windows
    for piece in range(pieces):
        w, part = piece // per_window, piece % per_window
        out_ref[piece] = turned[16 * w : 16 * w + 16, part * lanes : (part + 1) * lanes]


def amplitude(grid, place, miller_h, miller_k, miller_l, total_x, total_y, pieces):
    rows_x, rows_y, depth = grid.shape
    windows = miller_h.shape[0]
    wide = 16 * windows
    vmem = pl.BlockSpec(memory_space=pltpu.VMEM)
    smem = pl.BlockSpec(memory_space=pltpu.SMEM)
    return pl.pallas_call(
        functools.partial(amplitude_body, total_x=total_x, total_y=total_y),
        in_specs=[smem, smem, smem, smem, vmem],
        out_specs=vmem,
        out_shape=jax.ShapeDtypeStruct((pieces, 16, 32 * wide // pieces), jnp.float32),
        scratch_shapes=[
            pltpu.VMEM((max(depth, 32 * rows_y, 32 * rows_x), 2 * wide), jnp.float32),
            pltpu.VMEM((2, 32, wide), jnp.float32),
            pltpu.VMEM((rows_x, rows_y, 2 * wide), jnp.float32),
            pltpu.VMEM((rows_x, 32, wide), jnp.float32),
            pltpu.VMEM((512, wide), jnp.float32),
        ],
        compiler_params=pltpu.CompilerParams(vmem_limit_bytes=40 << 20),
    )(place, miller_h, miller_k, miller_l, grid)


def with_margins(cells, axis, dim):
    count = lax.axis_size(axis)
    length = cells.shape[dim] - 8
    head = lax.slice_in_dim(cells, 0, 4, axis=dim)
    tail = lax.slice_in_dim(cells, length + 4, length + 8, axis=dim)
    before = lax.ppermute(tail, axis, [(i, (i + 1) % count) for i in range(count)])
    after = lax.ppermute(head, axis, [((i + 1) % count, i) for i in range(count)])
    inner = lax.slice_in_dim(cells, 4, length + 4, axis=dim)
    parts = [lax.slice_in_dim(inner, 0, 4, axis=dim) + before]
    if length > 8:
        parts.append(lax.slice_in_dim(inner, 4, length - 4, axis=dim))
    parts.append(lax.slice_in_dim(inner, length - 4, length, axis=dim) + after)
    return jnp.concatenate(parts, axis=dim)


def shards(atom_cell, atom_frac, atom_weight, block_count, miller_h, miller_k, miller_l):
    blocks_x, blocks_y, blocks_z, _ = atom_weight.shape
    count_x, count_y = lax.axis_size("gx"), lax.axis_size("gy")
    width_x, width_y, depth = 8 * blocks_x, 8 * blocks_y, 8 * blocks_z
    total_x, total_y = width_x * count_x, width_y * count_y
    grid = deposit(atom_cell, atom_frac, atom_weight, block_count)
    place = jnp.stack([lax.axis_index("gx") * width_x - 4, lax.axis_index("gy") * width_y - 4])
    pieces = count_x * count_y
    waves = amplitude(
        grid, place.astype(jnp.int32), miller_h, miller_k, miller_l, total_x, total_y, pieces
    )
    waves = lax.all_to_all(waves, ("gx", "gy"), 0, 0, tiled=False)
    rows = miller_h.shape[0] * 16 // pieces
    summed = jnp.sum(waves, axis=0).reshape(16, rows, 2, 16)
    power = jnp.sum(summed * summed, axis=2) / float(total_x * total_y * depth)
    intensity = jnp.transpose(power, (1, 2, 0)).reshape(rows, 256)
    density = with_margins(with_margins(grid, "gx", 0), "gy", 1)
    return (density, intensity)


def solution(mesh):
    in_specs = (
        P(None, "gx", "gy", None, None),
        P(None, "gx", "gy", None, None),
        P("gx", "gy", None, None),
        P("gx", "gy", None),
        P(),
        P(),
        P(),
    )
    out_specs = (P("gx", "gy", None), P(("gx", "gy"), None))
    return jax.shard_map(shards, mesh=mesh, in_specs=in_specs, out_specs=out_specs, check_vma=False)
```

time: 395 us -> 82.8 us (0.21)
  local copies, waits for them, and re-layouts: 137 us -> 9.43 us
  waiting for transfers between devices: 131 us -> 21.9 us
  other arithmetic: 55.8 us -> 1.38 us
  matrix products: 41.7 us -> 0 us
  Pallas kernels: 0 us -> 41.1 us
  between operations: 14.3 us -> 0.8 us
  loops' own time: 4.02 us -> 0 us
    unnamed x2 -> x0, waiting for transfers between devices: 124 us -> none
    convert_element_type x2 -> x0, local copies, waits for them, and re-layouts: 92.8 us -> none  [footprints(): crossed = (taps_x[..., :, None] * taps_y[..., None, :]).reshape(blocks, c...]
    dot_general x11 -> x0, matrix products: 41.7 us -> none  [the longest x2 30 us: footprints(): jnp.einsum('bpc,bpm->bcm', scaled, crossed, preferred_element_type=jnp.fl...]
    pallas_call x0 -> x2, Pallas kernels: none -> 41.1 us  [the longest x1 36.9 us: deposit(): pl.pallas_call(body, grid=(by, bz // 16), in_specs=[pl.BlockSpec(memory_s...]
    convert_element_type x2 -> x0, other arithmetic: 30.8 us -> none  [footprints(): crossed = (taps_x[..., :, None] * taps_y[..., None, :]).reshape(blocks, c...]
    select_n x4 -> x0, local copies, waits for them, and re-layouts: 24.4 us -> none  [kernel_taps(): return jnp.where(inside, values, jnp.zeros_like(values))]
    select_n x3 -> x0, other arithmetic: 13.9 us -> none  [the longest x2 13.9 us: kernel_taps(): return jnp.where(inside, values, jnp.zeros_like(values))]
    all_to_all x0 -> x1, waiting for transfers between devices: none -> 9.03 us  [shards(): waves = lax.all_to_all(waves, ('gx', 'gy'), 0, 0, tiled=False)]
  transfers between devices with their start and end apart: 5 -> 5, of which waited for: 3 -> 3; matrix products, arithmetic and copies ran while one was open for 2% -> 1% of each run, Pallas kernels for 0% -> 5%
where the time goes in v1:
time: 82.8 us; the launch traced here: 82.5 us
  Pallas kernels  41.1 us (50%)
  waiting for transfers between devices  21.9 us (26%)
  local copies, waits for them, and re-layouts  9.43 us (11%)
  starting transfers between devices  7.9 us (10%)
  other arithmetic  1.38 us (2%)
    pallas_call x1, Pallas kernels, deposit(): pl.pallas_call(body, grid=(by, bz // 16), in_specs=[pl.BlockSpec(memory_s...  36.9 us
    ppermute x2, waiting for transfers between devices, with_margins(): lax.ppermute(tail, axis, [(i, (i + 1) % count) for i in range(count)])  9.5 us
    all_to_all x1, waiting for transfers between devices, shards(): waves = lax.all_to_all(waves, ('gx', 'gy'), 0, 0, tiled=False)  9.03 us
    unnamed x17, local copies, waits for them, and re-layouts  8.51 us
    all_to_all x1, starting transfers between devices, shards(): waves = lax.all_to_all(waves, ('gx', 'gy'), 0, 0, tiled=False)  4.64 us
    pallas_call x1, Pallas kernels, amplitude(): pl.pallas_call(functools.partial(amplitude_body, total_x=total_x, total_y...  4.21 us
    ppermute x2, waiting for transfers between devices, with_margins(): lax.ppermute(head, axis, [((i + 1) % count, i) for i in range(count)])  3.36 us
    ppermute x2, starting transfers between devices, with_margins(): lax.ppermute(tail, axis, [(i, (i + 1) % count) for i in range(count)])  2.32 us
  transfers between devices with their start and end apart: 5, of which 3 were waited for; matrix products, arithmetic and copies ran while one was open for 1% of the time, Pallas kernels for 5%

profile of v1, /device:TPU:0, one launch (start us, length us, event | category | flops | bytes accessed | tf_op | source)
XLA Modules:
  0.0 82.5 jit_solution(6167294083628574864)
XLA Ops:
  0.6 1.9 %copy.15.cell_ref = s32[3,1,2,128,576]{4,3,2,1,0:T(8,128)S(1)} copy(s32[3,1,2,128,576]{3,4,2,1,0:T(8,128)} %param.7) | data formatting | bytes 3538944 | tf_op args[0]
  2.5 0.0 copy-start.6
  2.5 0.0 copy-start.2
  2.5 2.9 %copy.16.frac_ref = f32[3,1,2,128,576]{4,3,2,1,0:T(8,128)} copy(f32[3,1,2,128,576]{3,4,2,1,0:T(8,128)} %param.8) | data formatting | bytes 3538944 | tf_op args[1]
  5.4 0.0 copy-done.6
  5.4 1.1 %copy.17.weight_ref = f32[1,2,128,576]{3,2,1,0:T(8,128)} copy(f32[1,2,128,576]{2,3,1,0:T(8,128)S(1)} %copy-done.6) | data formatting | bytes 1179648 | tf_op args[2]
  6.5 0.0 copy-done.2
  6.5 0.0 copy-start
  6.5 1.5 %copy-done = f32[3,1,2,128,576]{4,3,2,1,0:T(8,128)S(1)} copy-done((f32[3,1,2,128,576]{4,3,2,1,0:T(8,128)S(1)}, f32[3,1,2,128,576]{4,3,2,1,0:T(8,128)}, u32[]{:S(2)}) %copy-start) | copy-done | bytes 1769496
  8.1 0.0 copy-start.1
  8.1 1.1 %copy-done.1 = f32[1,2,128,576]{3,2,1,0:T(8,128)S(1)} copy-done((f32[1,2,128,576]{3,2,1,0:T(8,128)S(1)}, f32[1,2,128,576]{3,2,1,0:T(8,128)}, u32[]{:S(2)}) %copy-start.1) | copy-done | bytes 589848
  9.1 36.9 %shard_map.86.grid_ref = f32[16,24,1024]{2,1,0:T(8,128)S(1)} custom-call(s32[1,2,128]{2,1,0:T(2,128)S(1)} %copy-done.2, s32[3,1,2,128,576]{4,3,2,1,0:T(8,128)S(1)} %copy.15.cell_ref, f32[3,1,2,128,576]{4,3,2,1,0:T(8,128)S(1)} %copy-done, f32[1,2,128,576]{3,2,1,0:T(8,128)S(1)} %copy-done.1), custom_call_target="tpu_custom_call" | custom-call | tf_op jit(solution)/shard_map/pallas_call | solution.py:81
  46.1 0.0 copy-start.3
  46.1 0.0 copy-start.4
  46.1 0.0 copy-start.5
  46.1 0.5 collective-permute-start
  46.6 9.5 %collective-permute-done = f32[4,24,1024]{2,1,0:T(8,128)S(1)} collective-permute-done((f32[4,24,1024]{2,1,0:T(8,128)S(1)}, f32[4,24,1024]{2,1,0:T(8,128)S(1)}, u32[]{:S(2)}, u32[]{:S(2)}) %collective-permute-start) | collective-permute-done | bytes 393248 | tf_op jit(solution)/shard_map/ppermute | solution.py:232
  56.1 0.1 slice_add_fusion.1
  56.2 0.1 collective-permute-start.1
  56.3 0.1 pad_add_fusion.place_ref
  56.4 0.0 copy-done.3
  56.4 0.0 copy-done.4
  56.4 0.0 copy-done.5
  56.4 4.2 %shard_map.87 = f32[32,16,128]{2,1,0:T(8,128)} custom-call(s32[2]{0:T(128)S(1)} %pad_add_fusion.place_ref, s32[8]{0:T(128)S(1)} %copy-done.3, s32[8]{0:T(128)S(1)} %copy-done.4, s32[8]{0:T(128)S(1)} %copy-done.5, f32[16,24,1024]{2,1,0:T(8,128)S(1)} %shard_map.86.grid_ref), custom_call_target="tpu_custom_call" | custom-call | tf_op jit(solution)/shard_map/pallas_call | solution.py:211
  60.6 4.6 %all-to-all-start = ((f32[32,16,128]{2,1,0:T(8,128)}), f32[32,16,128]{2,1,0:T(8,128)S(1)}, u32[]{:S(2)}, u32[]{:S(2)}) async-start(f32[32,16,128]{2,1,0:T(8,128)} %shard_map.87), calls=%async_computation | async-start | bytes 524288 | tf_op jit(solution)/shard_map/all_to_all | solution.py:253
  65.3 0.0 collective-permute-done.1
  65.4 1.8 %collective-permute-start.2 = (f32[8,4,1024]{2,1,0:T(4,128)S(1)}, f32[8,4,1024]{2,1,0:T(4,128)S(1)}, u32[]{:S(2)}, u32[]{:S(2)}) collective-permute-start(f32[8,4,1024]{2,1,0:T(4,128)S(1)} %pad_maximum_fusion.2), channel_id=1, source_target_pairs={{0,1},{1,2},{2,3},{3,0},{4,5},{5,6},{6,7},{7,4},{8,9},{9,10},{10,1... | collective-permute-start | bytes 393224 | tf_op jit(solution)/shard_map/ppermute | solution.py:232
  67.2 9.0 %all-to-all-done = f32[32,16,128]{2,1,0:T(8,128)S(1)} async-done(((f32[32,16,128]{2,1,0:T(8,128)}), f32[32,16,128]{2,1,0:T(8,128)S(1)}, u32[]{:S(2)}, u32[]{:S(2)}) %all-to-all-start) | async-done | bytes 262176 | tf_op jit(solution)/shard_map/all_to_all | solution.py:253
  76.3 0.1 mul.15
  76.4 0.1 reduce_sum.19
  76.5 0.0 collective-permute-done.2
  76.5 0.1 maximum_add_fusion
  76.6 0.9 %collective-permute-start.3 = (f32[8,4,1024]{2,1,0:T(4,128)S(1)}, f32[8,4,1024]{2,1,0:T(4,128)S(1)}, u32[]{:S(2)}, u32[]{:S(2)}) collective-permute-start(f32[8,4,1024]{2,1,0:T(4,128)S(1)} %get-tuple-element.5), channel_id=1, source_target_pairs={{1,0},{2,1},{3,2},{0,3},{5,4},{6,5},{7,6},{4,7},{9,8},{10,9},{11,1... | collective-permute-start | bytes 393224 | tf_op jit(solution)/shard_map/ppermute | solution.py:233
  77.5 0.1 copy.19
  77.5 0.7 reshape.9
  78.2 3.4 %collective-permute-done.3 = f32[8,4,1024]{2,1,0:T(4,128)S(1)} collective-permute-done((f32[8,4,1024]{2,1,0:T(4,128)S(1)}, f32[8,4,1024]{2,1,0:T(4,128)S(1)}, u32[]{:S(2)}, u32[]{:S(2)}) %collective-permute-start.3) | collective-permute-done | bytes 131104 | tf_op jit(solution)/shard_map/ppermute | solution.py:233
  81.6 0.9 %pad_maximum_fusion = f32[8,16,1024]{2,1,0:T(8,128)} fusion(f32[8,4,1024]{2,1,0:T(4,128)S(1)} %fusion.2, f32[8,8,1024]{2,1,0:T(8,128)S(1)} %fusion, f32[8,4,1024]{2,1,0:T(4,128)S(1)} %get-tuple-element.4), kind=kLoop, calls=%fused_computation.4 | loop fusion | flops 262144 | bytes 1048576 | tf_op jit(solution)/shard_map/concatenate | solution.py:239
  (8 shorter events, 0.2 us)
Async XLA Ops:
  2.5 2.9 %copy-start.6 = (f32[1,2,128,576]{2,3,1,0:T(8,128)S(1)}, f32[1,2,128,576]{2,3,1,0:T(8,128)}, u32[]{:S(2)}) copy-start(f32[1,2,128,576]{2,3,1,0:T(8,128)} %param.9) | copy-start | bytes 1769476
  2.5 4.0 %copy-start.2 = (s32[1,2,128]{2,1,0:T(2,128)S(1)}, s32[1,2,128]{2,1,0:T(2,128)}, u32[]{:S(2)}) copy-start(s32[1,2,128]{2,1,0:T(2,128)} %count_ref.1) | copy-start | bytes 3076
  6.5 1.5 %copy-start = (f32[3,1,2,128,576]{4,3,2,1,0:T(8,128)S(1)}, f32[3,1,2,128,576]{4,3,2,1,0:T(8,128)}, u32[]{:S(2)}) copy-start(f32[3,1,2,128,576]{4,3,2,1,0:T(8,128)} %copy.16.frac_ref) | copy-start | bytes 5308420
  8.1 1.1 %copy-start.1 = (f32[1,2,128,576]{3,2,1,0:T(8,128)S(1)}, f32[1,2,128,576]{3,2,1,0:T(8,128)}, u32[]{:S(2)}) copy-start(f32[1,2,128,576]{3,2,1,0:T(8,128)} %copy.17.weight_ref) | copy-start | bytes 1769476
  46.1 10.3 %copy-start.3 = (s32[8]{0:T(128)S(1)}, s32[8]{0:T(128)}, u32[]{:S(2)}) copy-start(s32[8]{0:T(128)} %h_ref.1) | copy-start | bytes 100
  46.1 10.3 %copy-start.4 = (s32[8]{0:T(128)S(1)}, s32[8]{0:T(128)}, u32[]{:S(2)}) copy-start(s32[8]{0:T(128)} %k_ref.1) | copy-start | bytes 100
  46.1 10.3 %copy-start.5 = (s32[8]{0:T(128)S(1)}, s32[8]{0:T(128)}, u32[]{:S(2)}) copy-start(s32[8]{0:T(128)} %l_ref.1) | copy-start | bytes 100
  46.1 10.0 %collective-permute-start = (f32[4,24,1024]{2,1,0:T(8,128)S(1)}, f32[4,24,1024]{2,1,0:T(8,128)S(1)}, u32[]{:S(2)}, u32[]{:S(2)}) collective-permute-start(f32[4,24,1024]{2,1,0:T(8,128)S(1)} %slice.44), channel_id=1, source_target_pairs={{0,4},{4,8},{8,12},{12,16},{16,20},{20,24},{24,28},{28,0},{1,5},{5... | collective-permute-start | bytes 1179656 | tf_op jit(solution)/shard_map/ppermute | solution.py:232
  56.2 9.0 %collective-permute-start.1 = (f32[4,24,1024]{2,1,0:T(8,128)S(1)}, f32[4,24,1024]{2,1,0:T(8,128)S(1)}, u32[]{:S(2)}, u32[]{:S(2)}) collective-permute-start(f32[4,24,1024]{2,1,0:T(8,128)S(1)} %get-tuple-element.3), channel_id=1, source_target_pairs={{4,0},{8,4},{12,8},{16,12},{20,16},{24,20},{28,24},{0,28},{5,1},{9... | collective-permute-start | bytes 1179656 | tf_op jit(solution)/shard_map/ppermute | solution.py:233
  60.6 15.6 %all-to-all-start = ((f32[32,16,128]{2,1,0:T(8,128)}), f32[32,16,128]{2,1,0:T(8,128)S(1)}, u32[]{:S(2)}, u32[]{:S(2)}) async-start(f32[32,16,128]{2,1,0:T(8,128)} %shard_map.87), calls=%async_computation | async-start | bytes 524288 | tf_op jit(solution)/shard_map/all_to_all | solution.py:253
  65.4 11.1 %collective-permute-start.2 = (f32[8,4,1024]{2,1,0:T(4,128)S(1)}, f32[8,4,1024]{2,1,0:T(4,128)S(1)}, u32[]{:S(2)}, u32[]{:S(2)}) collective-permute-start(f32[8,4,1024]{2,1,0:T(4,128)S(1)} %pad_maximum_fusion.2), channel_id=1, source_target_pairs={{0,1},{1,2},{2,3},{3,0},{4,5},{5,6},{6,7},{7,4},{8,9},{9,10},{10,1... | collective-permute-start | bytes 393224 | tf_op jit(solution)/shard_map/ppermute | solution.py:232
  76.6 5.0 %collective-permute-start.3 = (f32[8,4,1024]{2,1,0:T(4,128)S(1)}, f32[8,4,1024]{2,1,0:T(4,128)S(1)}, u32[]{:S(2)}, u32[]{:S(2)}) collective-permute-start(f32[8,4,1024]{2,1,0:T(4,128)S(1)} %get-tuple-element.5), channel_id=1, source_target_pairs={{1,0},{2,1},{3,2},{0,3},{5,4},{6,5},{7,6},{4,7},{9,8},{10,9},{11,1... | collective-permute-start | bytes 393224 | tf_op jit(solution)/shard_map/ppermute | solution.py:233

commit v2 on v1

v2 whole, which is shorter than its diff:
```python
import functools
import math
import jax, jax.numpy as jnp
from jax import lax
from jax.experimental import pallas as pl
from jax.experimental.pallas import tpu as pltpu
from jax.sharding import PartitionSpec as P
KERNEL_SIGMA=0.9
NORMAL=1.0/(KERNEL_SIGMA*math.sqrt(2.0*math.pi))
NT=(((1,),(1,)),((),()))
SCALE=math.sqrt(0.5/math.log(2.0))/KERNEL_SIGMA
LOGN=math.log2(NORMAL)
UNROLL=8
FAR=-1.0e4
def deposit_body(count_ref,cell_ref,frac_ref,weight_ref,head_ref,mid_ref,tail_ref,rows_ref,edge_ref,line_ref):
    column=pl.program_id(0)
    cap,blocks_z=cell_ref.shape[3:]
    depth=8*blocks_z; half=blocks_z//2; two=2*cap
    line_ref[...]=jnp.zeros_like(line_ref)
    def paired(v):
        v=jnp.transpose(v)
        return jnp.concatenate([v[0:half],v[half:]],axis=1).reshape(half//8,8,two)
    for d in range(3):
        cell=cell_ref[d,0,0].astype(jnp.float32)
        place=cell+frac_ref[d,0,0]
        if d==0:
            upper=jnp.where(cell>3.5,1.0,0.0)
            rows_ref[0]=paired((place-3.5)*SCALE)
            rows_ref[1]=paired(upper)
            rows_ref[2]=paired(cell-4.0*upper)
        else:
            rows_ref[2*d+1]=paired(place*SCALE)
            rows_ref[2*d+2]=paired(cell)
    slots=lax.broadcasted_iota(jnp.int32,(cap,blocks_z),0)
    rows_ref[7]=paired(jnp.where(slots<count_ref[0,pl.ds(column,1),:],weight_ref[0,0],0.0))
    row=lax.broadcasted_iota(jnp.int32,(8,128),0)
    r8=row.astype(jnp.float32)
    low=(r8-4.0)*SCALE; high=(r8+4.0)*SCALE
    r4=(row%4).astype(jnp.float32)
    second=row>=4
    nodes=(4.0*r4-6.0)*SCALE
    first=jnp.where(second,1.0,0.0)
    on0=jnp.where((r4>=first)&(r4<=first+1.0),0.0,FAR)
    on1=jnp.where((r4>=first+1.0)&(r4<=first+2.0),0.0,FAR)
    slopes=(r4-1.5)*(2.0*SCALE)
    sign=jnp.where(second,-1.0,1.0)
    bound=jnp.where(second,0.5-r4,r4)
    part=cap%128
    lanes=lax.broadcasted_iota(jnp.int32,(16,128),1)
    zero=jnp.zeros((16,128),jnp.float32)
    def group(g,carry):
        for u in range(UNROLL):
            slot=u%2
            i=g*UNROLL+u
            acc=[None,None]
            for t in range(two//128):
                def line(k): return rows_ref[k,g,u:u+1,128*t:128*t+128]
                rx=line(0)
                q=rx-nodes
                here=slot*(two//128)+t
                edge_ref[here,0:8]=jnp.exp2(jnp.where(line(1)>0.5,on1,on0)-q*q)
                edge_ref[here,8:16]=jnp.exp2(jnp.where(bound>sign*line(2),slopes*rx,FAR))
                def taps(d):
                    inside=r8>line(2*d+2)
                    dist=jnp.where(inside,low,high)-line(2*d+1)
                    return inside,jnp.exp2(LOGN-dist*dist)
                my,vy=taps(1)
                y=jnp.concatenate([jnp.where(my,vy,0.0),jnp.where(my,0.0,vy)],axis=0)
                mz,vz=taps(2); vz=vz*line(7)
                z=jnp.concatenate([jnp.where(mz,vz,0.0),jnp.where(mz,0.0,vz)],axis=0)
                def rows(values,first):
                    return jnp.concatenate([jnp.concatenate([(values*edge_ref[here,first+4*s+h:first+4*s+h+1,:]).astype(jnp.bfloat16) for h in range(4)],axis=0) for s in range(2)],axis=1)
                right=rows(y,8)
                if part and t==cap//128: sides=[(0,jnp.where(lanes<part,z,0.0)),(1,jnp.where(lanes<part,0.0,z))]
                else: sides=[(int(128*t>=cap),z)]
                for side,values in sides:
                    more=lax.dot_general(rows(values,0),right,NT,preferred_element_type=jnp.float32)
                    acc[side]=more if acc[side] is None else acc[side]+more
            base=pl.multiple_of(8*i,8)
            for s in range(2):
                for h in range(4):
                    line_ref[h,pl.ds(base+8*half*s,16),:]+=acc[s][16*h:16*h+16]
        return carry
    lax.fori_loop(0,half//UNROLL,group,0)
    outs=(head_ref,mid_ref,tail_ref)
    @pl.when(column==0)
    def _():
        for ref in outs: ref[...]=jnp.zeros_like(ref)
    for h in range(4):
        line_ref[h,4:8,:]+=line_ref[h,depth+4:depth+8,:]
        line_ref[h,depth:depth+4,:]+=line_ref[h,0:4,:]
    at=pl.ds(pl.multiple_of(8*column,8),16)
    for h in range(4):
        for c in range(depth//128):
            turned=jnp.transpose(line_ref[h,128*c+4:128*c+132,:])
            for k in range(4):
                near=k-1.5
                factor=NORMAL*math.exp((-near*(4*h-6)-0.5*near*near)/KERNEL_SIGMA**2)
                ref=outs[(h+1)//2]
                place=k if h!=2 else 4+k
                ref[place,at,128*c:128*c+128]+=turned[16*k:16*k+16]*factor

def deposit(cell,frac,weight,count):
    _,bx,by,bz,cap=cell.shape
    span=-(-cap//128)*128
    swap=lambda v: jnp.swapaxes(v,-1,-2)
    return pl.pallas_call(deposit_body,
        grid=(by,),
        in_specs=[pl.BlockSpec((1,by,bz),lambda j:(0,0,0)),
                  pl.BlockSpec((3,1,1,cap,bz),lambda j:(0,0,j,0,0)),
                  pl.BlockSpec((3,1,1,cap,bz),lambda j:(0,0,j,0,0)),
                  pl.BlockSpec((1,1,cap,bz),lambda j:(0,j,0,0))],
        out_specs=[pl.BlockSpec((n,8*by+8,8*bz),lambda j:(0,0,0)) for n in (4,8,4)],
        out_shape=[jax.ShapeDtypeStruct((n,8*by+8,8*bz),jnp.float32) for n in (4,8,4)],
        scratch_shapes=[pltpu.VMEM((8,bz//16,8,2*cap),jnp.float32),pltpu.VMEM((2*(2*cap//128),16,128),jnp.float32),
                        pltpu.VMEM((4,8*bz+8,64),jnp.float32)],
        compiler_params=pltpu.CompilerParams(vmem_limit_bytes=62<<20),
    )(count,swap(cell),swap(frac),swap(weight))


def turn(freqs, place, extent):
    product = freqs * place
    if extent & (extent - 1) == 0:
        product = product & (extent - 1)
    else:
        product = lax.rem(lax.rem(product, extent) + extent, extent)
    angle = product.astype(jnp.float32) * (2.0 * math.pi / extent)
    return jnp.cos(angle), jnp.sin(angle)


def times(one, other):
    return (
        one[0] * other[0] - one[1] * other[1],
        one[0] * other[1] + one[1] * other[0],
    )


def split(value):
    head = value.astype(jnp.bfloat16)
    return head, (value - head.astype(jnp.float32)).astype(jnp.bfloat16)


def amplitude_body(
    place_ref, h_ref, k_ref, l_ref, head_ref, mid_ref, tail_ref, out_ref,
    phase_ref, shift_ref, along_z_ref, half_ref, wave_ref, *, total_x, total_y
):
    rows_x, rows_y, _ = along_z_ref.shape
    depth = mid_ref.shape[2]
    windows = h_ref.shape[0]
    wide = 16 * windows

    def centres(ref, shape):
        window = lax.broadcasted_iota(jnp.int32, shape, 1) // 16
        found = jnp.zeros(shape, jnp.int32)
        for w in range(windows):
            found = jnp.where(window == w, ref[w], found)
        return found

    block = 32
    below = lax.broadcasted_iota(jnp.int32, (block, wide), 0)
    freq_l = centres(l_ref, (block, wide)) + lax.rem(lax.broadcasted_iota(jnp.int32, (block, wide), 1), 16) - 8
    fine = turn(freq_l, below, depth)
    coarse = turn(freq_l, below * block, depth)
    shift_ref[0] = coarse[0]
    shift_ref[1] = coarse[1]
    for step in range(depth // block):
        now = times(fine, (shift_ref[0, step : step + 1], shift_ref[1, step : step + 1]))
        at = pl.ds(step * block, block)
        phase_ref[at, 0:wide] = now[0]
        phase_ref[at, wide : 2 * wide] = -now[1]
    table, left = split(phase_ref[0:depth])

    def dot(a, b):
        return jnp.dot(a, b, preferred_element_type=jnp.float32)

    start = 0
    for ref in (head_ref, mid_ref, tail_ref):
        count = ref.shape[0]
        value, rest = split(ref[...].reshape(count * rows_y, depth))
        found = dot(value, table) + (dot(value, left) + dot(rest, table))
        along_z_ref[start : start + count] = found.reshape(count, rows_y, 2 * wide)
        start += count
    row16 = lax.broadcasted_iota(jnp.int32, (16, wide), 0)
    freq_k = centres(k_ref, (16, wide)) + row16 - 8
    now = turn(freq_k, place_ref[1] + 2 * total_y, total_y)
    step = turn(freq_k, 1, total_y)
    for y in range(rows_y):
        phase_ref[pl.ds(32 * y, 16), 0:wide] = now[0]
        phase_ref[pl.ds(32 * y + 16, 16), 0:wide] = now[1]
        now = times(now, step)
    group = 4
    for x in range(0, rows_x, group):
        real = [jnp.zeros((16, wide), jnp.float32)] * group
        imag = [jnp.zeros((16, wide), jnp.float32)] * group
        for y in range(rows_y):
            cos = phase_ref[pl.ds(32 * y, 16), 0:wide]
            sin = phase_ref[pl.ds(32 * y + 16, 16), 0:wide]
            for g in range(group):
                a = along_z_ref[x + g, y : y + 1, 0:wide]
                b = along_z_ref[x + g, y : y + 1, wide : 2 * wide]
                real[g] = real[g] + (a * cos + b * sin)
                imag[g] = imag[g] + (b * cos - a * sin)
        for g in range(group):
            half_ref[x + g, 0:16] = real[g]
            half_ref[x + g, 16:32] = imag[g]
    freq_h = centres(h_ref, (16, wide)) + row16 - 8
    now = turn(freq_h, place_ref[0] + 2 * total_x, total_x)
    step = turn(freq_h, 1, total_x)
    for x in range(rows_x):
        phase_ref[pl.ds(32 * x, 16), wide : 2 * wide] = now[0]
        phase_ref[pl.ds(32 * x + 16, 16), wide : 2 * wide] = now[1]
        now = times(now, step)
    for h in range(0, 16, group):
        real = [jnp.zeros((16, wide), jnp.float32)] * group
        imag = [jnp.zeros((16, wide), jnp.float32)] * group
        for x in range(rows_x):
            a = half_ref[x, 0:16]
            b = half_ref[x, 16:32]
            for g in range(group):
                cos = phase_ref[32 * x + h + g : 32 * x + h + g + 1, wide : 2 * wide]
                sin = phase_ref[32 * x + 16 + h + g : 32 * x + 17 + h + g, wide : 2 * wide]
                real[g] = real[g] + (a * cos + b * sin)
                imag[g] = imag[g] + (b * cos - a * sin)
        for g in range(group):
            wave_ref[pl.ds(32 * (h + g), 16)] = real[g]
            wave_ref[pl.ds(32 * (h + g) + 16, 16)] = imag[g]
    turned = jnp.transpose(wave_ref[...])
    pieces, _, lanes = out_ref.shape
    per_window = pieces // windows
    for piece in range(pieces):
        w, part = piece // per_window, piece % per_window
        out_ref[piece] = turned[16 * w : 16 * w + 16, part * lanes : (part + 1) * lanes]


def amplitude(grids, place, miller_h, miller_k, miller_l, total_x, total_y, pieces):
    _, rows_y, depth = grids[0].shape
    rows_x = sum(grid.shape[0] for grid in grids)
    windows = miller_h.shape[0]
    wide = 16 * windows
    vmem = pl.BlockSpec(memory_space=pltpu.VMEM)
    smem = pl.BlockSpec(memory_space=pltpu.SMEM)
    return pl.pallas_call(
        functools.partial(amplitude_body, total_x=total_x, total_y=total_y),
        in_specs=[smem, smem, smem, smem, vmem, vmem, vmem],
        out_specs=vmem,
        out_shape=jax.ShapeDtypeStruct((pieces, 16, 32 * wide // pieces), jnp.float32),
        scratch_shapes=[
            pltpu.VMEM((max(depth, 32 * rows_y, 32 * rows_x), 2 * wide), jnp.float32),
            pltpu.VMEM((2, 32, wide), jnp.float32),
            pltpu.VMEM((rows_x, rows_y, 2 * wide), jnp.float32),
            pltpu.VMEM((rows_x, 32, wide), jnp.float32),
            pltpu.VMEM((512, wide), jnp.float32),
        ],
        compiler_params=pltpu.CompilerParams(vmem_limit_bytes=40 << 20),
        cost_estimate=pl.CostEstimate(flops=5_000_000_000, bytes_accessed=8_000_000, transcendentals=100_000),
    )(place, miller_h, miller_k, miller_l, *grids)


def exchange(head, tail, axis):
    count = lax.axis_size(axis)
    before = lax.ppermute(tail, axis, [(i, (i + 1) % count) for i in range(count)])
    after = lax.ppermute(head, axis, [((i + 1) % count, i) for i in range(count)])
    return before, after


def added(inner, before, after, dim):
    length = inner.shape[dim]
    widths = [(0, 0)] * inner.ndim
    widths[dim] = (0, length - 4)
    leading = jnp.pad(before, widths)
    widths[dim] = (length - 4, 0)
    return inner + leading + jnp.pad(after, widths)


def shards(atom_cell, atom_frac, atom_weight, block_count, miller_h, miller_k, miller_l):
    blocks_x, blocks_y, blocks_z, _ = atom_weight.shape
    count_x, count_y = lax.axis_size("gx"), lax.axis_size("gy")
    width_x, width_y, depth = 8 * blocks_x, 8 * blocks_y, 8 * blocks_z
    total_x, total_y = width_x * count_x, width_y * count_y
    place = jnp.stack([lax.axis_index("gx") * width_x - 4, lax.axis_index("gy") * width_y - 4])
    grids = deposit(atom_cell, atom_frac, atom_weight, block_count)
    head, mid, tail = grids
    before, after = exchange(head, tail, "gx")
    pieces = count_x * count_y
    waves = amplitude(
        grids, place.astype(jnp.int32), miller_h, miller_k, miller_l, total_x, total_y, pieces
    )
    before, after, _ = lax.optimization_barrier((before, after, waves))
    received = lax.all_to_all(waves, ("gx", "gy"), 0, 0, tiled=False)
    rows = miller_h.shape[0] * 16 // pieces
    summed = jnp.sum(received, axis=0).reshape(16, rows, 2, 16)
    power = jnp.sum(summed * summed, axis=2) / float(total_x * total_y * depth)
    intensity = jnp.transpose(power, (1, 2, 0)).reshape(rows, 256)
    wide = added(mid, before, after, 0)
    before, after = exchange(wide[:, :4], wide[:, width_y + 4 :], "gy")
    density = added(wide[:, 4 : width_y + 4], before, after, 1)
    return (density, intensity)


def solution(mesh):
    in_specs = (
        P(None, "gx", "gy", None, None),
        P(None, "gx", "gy", None, None),
        P("gx", "gy", None, None),
        P("gx", "gy", None),
        P(),
        P(),
        P(),
    )
    out_specs = (P("gx", "gy", None), P(("gx", "gy"), None))
    return jax.shard_map(shards, mesh=mesh, in_specs=in_specs, out_specs=out_specs, check_vma=False)
```

time: 82.8 us -> 55.5 us (0.67)
  waiting for transfers between devices: 21.9 us -> 7.88 us
  Pallas kernels: 41.1 us -> 29.3 us
  local copies, waits for them, and re-layouts: 9.43 us -> 4.07 us
  starting transfers between devices: 7.9 us -> 12 us
    ppermute x4, waiting for transfers between devices: 12.9 us -> 0.01 us  [the longest x2 0.01 us: exchange(): lax.ppermute(tail, axis, [(i, (i + 1) % count) for i in range(count)])]
    pallas_call x1, Pallas kernels: 36.9 us -> 25.1 us  [deposit(): pl.pallas_call(deposit_body, grid=(by,), in_specs=[pl.BlockSpec((1, by, b...]
    unnamed x17 -> x14, local copies, waits for them, and re-layouts: 8.51 us -> 3.14 us
    ppermute x4, starting transfers between devices: 3.26 us -> 7.47 us  [the longest x2 5.2 us: exchange(): lax.ppermute(head, axis, [((i + 1) % count, i) for i in range(count)])]
    all_to_all x1, waiting for transfers between devices: 9.03 us -> 7.87 us  [shards(): received = lax.all_to_all(waves, ('gx', 'gy'), 0, 0, tiled=False)]
    concatenate x2 -> x0, other arithmetic: 0.91 us -> none  [with_margins(): return jnp.concatenate(parts, axis=dim)]
  transfers between devices with their start and end apart: 5 -> 5, of which waited for: 3 -> 1; matrix products, arithmetic and copies ran while one was open for 1% -> 2% of each run, Pallas kernels for 5% -> 8%
where the time goes in v2:
time: 55.5 us; the launch traced here: 55.2 us
  Pallas kernels  29.3 us (53%)
  starting transfers between devices  12 us (22%)
  waiting for transfers between devices  7.88 us (14%)
  local copies, waits for them, and re-layouts  4.07 us (7%)
  other arithmetic  1.23 us (2%)
  between operations  0.74 us (1%)
    pallas_call x1, Pallas kernels, deposit(): pl.pallas_call(deposit_body, grid=(by,), in_specs=[pl.BlockSpec((1, by, b...  25.1 us
    all_to_all x1, waiting for transfers between devices, shards(): received = lax.all_to_all(waves, ('gx', 'gy'), 0, 0, tiled=False)  7.87 us
    ppermute x2, starting transfers between devices, exchange(): lax.ppermute(head, axis, [((i + 1) % count, i) for i in range(count)])  5.2 us
    all_to_all x1, starting transfers between devices, shards(): received = lax.all_to_all(waves, ('gx', 'gy'), 0, 0, tiled=False)  4.53 us
    pallas_call x1, Pallas kernels, amplitude(): pl.pallas_call(functools.partial(amplitude_body, total_x=total_x, total_y...  4.18 us
    unnamed x14, local copies, waits for them, and re-layouts  3.14 us
    ppermute x2, starting transfers between devices, exchange(): lax.ppermute(tail, axis, [(i, (i + 1) % count) for i in range(count)])  2.27 us
  transfers between devices with their start and end apart: 5, of which 1 were waited for; matrix products, arithmetic and copies ran while one was open for 2% of the time, Pallas kernels for 8%

profile of v2, /device:TPU:0, one launch (start us, length us, event | category | flops | bytes accessed | tf_op | source)
XLA Modules:
  0.0 55.2 jit_solution(420688745335236606)
XLA Ops:
  0.6 0.0 copy-start.4
  0.6 0.0 copy-start.5
  0.7 0.0 copy-start.6
  0.7 25.1 %shard_map.86 = (f32[4,24,1024]{2,1,0:T(8,128)}, f32[8,24,1024]{2,1,0:T(8,128)}, f32[4,24,1024]{2,1,0:T(8,128)}) custom-call(s32[1,2,128]{2,1,0:T(2,128)} %count_ref.1, s32[3,1,2,576,128]{4,3,2,1,0:T(8,128)} %bitcast.7, f32[3,1,2,576,128]{4,3,2,1,0:T(8,128)} %bitcast.8, f32[1,2,576,128]{3,2,1,0:T(8,128)} %bitcast.9), custom_call_target="tpu_custom_call" | custom-call | tf_op jit(solution)/shard_map/pallas_call | solution.py:107
  25.7 0.5 collective-permute-start
  26.2 4.0 %collective-permute-start.1 = (f32[4,24,1024]{2,1,0:T(8,128)}, f32[4,24,1024]{2,1,0:T(8,128)S(1)}, u32[]{:S(2)}, u32[]{:S(2)}) collective-permute-start(f32[4,24,1024]{2,1,0:T(8,128)} %get-tuple-element.9.head_ref), channel_id=1, source_target_pairs={{4,0},{8,4},{12,8},{16,12},{20,16},{24,20},{28,24},{0,28},{5,1},{9... | collective-permute-start | bytes 1179656 | tf_op jit(solution)/shard_map/ppermute | solution.py:262
  30.2 0.1 pad_add_fusion.1.place_ref
  30.3 0.0 copy-done.4
  30.3 0.0 copy-done.5
  30.3 0.0 copy-done.6
  30.3 0.0 copy-start
  30.3 1.1 %copy-done = f32[8,24,1024]{2,1,0:T(8,128)S(1)} copy-done((f32[8,24,1024]{2,1,0:T(8,128)S(1)}, f32[8,24,1024]{2,1,0:T(8,128)}, u32[]{:S(2)}) %copy-start) | copy-done | bytes 786456
  31.5 0.0 copy-start.2
  31.5 1.0 %copy-done.2 = f32[4,24,1024]{2,1,0:T(8,128)S(1)} copy-done((f32[4,24,1024]{2,1,0:T(8,128)S(1)}, f32[4,24,1024]{2,1,0:T(8,128)}, u32[]{:S(2)}) %copy-start.2) | copy-done | bytes 393240
  32.5 0.0 copy-start.3
  32.5 1.0 %copy-done.3 = f32[4,24,1024]{2,1,0:T(8,128)S(1)} copy-done((f32[4,24,1024]{2,1,0:T(8,128)S(1)}, f32[4,24,1024]{2,1,0:T(8,128)}, u32[]{:S(2)}) %copy-start.3) | copy-done | bytes 393240
  33.5 0.0 copy-start.1
  33.5 4.2 %shard_map.87 = f32[32,16,128]{2,1,0:T(8,128)} custom-call(s32[2]{0:T(128)S(1)} %pad_add_fusion.1.place_ref, s32[8]{0:T(128)S(1)} %copy-done.4, s32[8]{0:T(128)S(1)} %copy-done.5, s32[8]{0:T(128)S(1)} %copy-done.6, f32[4,24,1024]{2,1,0:T(8,128)S(1)} %copy-done.2, f32[8,24,1024]{2,1,0:T(8,128)S(1)} %copy-done, f32[4,24,1024]{2,1,0:T(8,128)S(1)} %copy-done.3), custom_call_target="tpu_custom_call" | custom-call | flops 5000000000 | bytes 8000000 | tf_op jit(solution)/shard_map/pallas_call | solution.py:242
  37.6 4.5 %all-to-all-start = ((f32[32,16,128]{2,1,0:T(8,128)}), f32[32,16,128]{2,1,0:T(8,128)S(1)}, u32[]{:S(2)}, u32[]{:S(2)}) async-start(f32[32,16,128]{2,1,0:T(8,128)} %shard_map.87), calls=%async_computation | async-start | bytes 524288 | tf_op jit(solution)/shard_map/all_to_all | solution.py:289
  42.2 0.0 collective-permute-done
  42.2 0.0 collective-permute-done.1
  42.2 0.0 copy-done.1
  42.2 0.1 pad_add_fusion
  42.3 0.1 fusion.2
  42.4 1.8 %collective-permute-start.2 = (f32[8,4,1024]{2,1,0:T(4,128)S(1)}, f32[8,4,1024]{2,1,0:T(4,128)S(1)}, u32[]{:S(2)}, u32[]{:S(2)}) collective-permute-start(f32[8,4,1024]{2,1,0:T(4,128)S(1)} %get-tuple-element.12), channel_id=1, source_target_pairs={{0,1},{1,2},{2,3},{3,0},{4,5},{5,6},{6,7},{7,4},{8,9},{9,10},{10,1... | collective-permute-start | bytes 393224 | tf_op jit(solution)/shard_map/ppermute | solution.py:261
  44.2 1.2 %collective-permute-start.3 = (f32[8,4,1024]{2,1,0:T(4,128)S(1)}, f32[8,4,1024]{2,1,0:T(4,128)S(1)}, u32[]{:S(2)}, u32[]{:S(2)}) collective-permute-start(f32[8,4,1024]{2,1,0:T(4,128)S(1)} %get-tuple-element.13), channel_id=1, source_target_pairs={{1,0},{2,1},{3,2},{0,3},{5,4},{6,5},{7,6},{4,7},{9,8},{10,9},{11,1... | collective-permute-start | bytes 393224 | tf_op jit(solution)/shard_map/ppermute | solution.py:262
  45.4 7.9 %all-to-all-done = f32[32,16,128]{2,1,0:T(8,128)S(1)} async-done(((f32[32,16,128]{2,1,0:T(8,128)}), f32[32,16,128]{2,1,0:T(8,128)S(1)}, u32[]{:S(2)}, u32[]{:S(2)}) %all-to-all-start) | async-done | bytes 262176 | tf_op jit(solution)/shard_map/all_to_all | solution.py:289
  53.3 0.1 mul.15
  53.4 0.1 reduce_sum.19
  53.5 0.1 copy.10
  53.6 0.7 %reshape.9 = f32[4,256]{1,0:T(4,128)} reshape(f32[4,16,16]{2,1,0:T(8,128)S(1)} %copy.10) | data formatting | bytes 8192 | tf_op jit(solution)/shard_map/reshape | solution.py:293
  54.3 0.0 collective-permute-done.2
  54.3 0.0 collective-permute-done.3
  54.3 0.9 %fusion = f32[8,16,1024]{2,1,0:T(8,128)} fusion(f32[8,24,1024]{2,1,0:T(8,128)S(1)} %pad_add_fusion, f32[8,4,1024]{2,1,0:T(4,128)S(1)} %collective-permute-done.3, f32[8,4,1024]{2,1,0:T(4,128)S(1)} %collective-permute-done.2), kind=kLoop, calls=%fused_computation.2 | loop fusion | flops 262144 | bytes 1310720 | tf_op jit(solution)/shard_map/add | solution.py:272
  (3 shorter events, 0.0 us)
Async XLA Ops:
  0.6 29.7 %copy-start.4 = (s32[8]{0:T(128)S(1)}, s32[8]{0:T(128)}, u32[]{:S(2)}) copy-start(s32[8]{0:T(128)} %h_ref.1) | copy-start | bytes 100
  0.6 29.7 %copy-start.5 = (s32[8]{0:T(128)S(1)}, s32[8]{0:T(128)}, u32[]{:S(2)}) copy-start(s32[8]{0:T(128)} %k_ref.1) | copy-start | bytes 100
  0.7 29.7 %copy-start.6 = (s32[8]{0:T(128)S(1)}, s32[8]{0:T(128)}, u32[]{:S(2)}) copy-start(s32[8]{0:T(128)} %l_ref.1) | copy-start | bytes 100
  25.7 16.4 %collective-permute-start = (f32[4,24,1024]{2,1,0:T(8,128)}, f32[4,24,1024]{2,1,0:T(8,128)S(1)}, u32[]{:S(2)}, u32[]{:S(2)}) collective-permute-start(f32[4,24,1024]{2,1,0:T(8,128)} %get-tuple-element.8.tail_ref), channel_id=1, source_target_pairs={{0,4},{4,8},{8,12},{12,16},{16,20},{20,24},{24,28},{28,0},{1,5},{5... | collective-permute-start | bytes 1179656 | tf_op jit(solution)/shard_map/ppermute | solution.py:261
  26.2 16.0 %collective-permute-start.1 = (f32[4,24,1024]{2,1,0:T(8,128)}, f32[4,24,1024]{2,1,0:T(8,128)S(1)}, u32[]{:S(2)}, u32[]{:S(2)}) collective-permute-start(f32[4,24,1024]{2,1,0:T(8,128)} %get-tuple-element.9.head_ref), channel_id=1, source_target_pairs={{4,0},{8,4},{12,8},{16,12},{20,16},{24,20},{28,24},{0,28},{5,1},{9... | collective-permute-start | bytes 1179656 | tf_op jit(solution)/shard_map/ppermute | solution.py:262
  30.3 1.1 %copy-start = (f32[8,24,1024]{2,1,0:T(8,128)S(1)}, f32[8,24,1024]{2,1,0:T(8,128)}, u32[]{:S(2)}) copy-start(f32[8,24,1024]{2,1,0:T(8,128)} %get-tuple-element.7.mid_ref) | copy-start | bytes 2359300
  31.5 1.0 %copy-start.2 = (f32[4,24,1024]{2,1,0:T(8,128)S(1)}, f32[4,24,1024]{2,1,0:T(8,128)}, u32[]{:S(2)}) copy-start(f32[4,24,1024]{2,1,0:T(8,128)} %get-tuple-element.9.head_ref) | copy-start | bytes 1179652
  32.5 1.0 %copy-start.3 = (f32[4,24,1024]{2,1,0:T(8,128)S(1)}, f32[4,24,1024]{2,1,0:T(8,128)}, u32[]{:S(2)}) copy-start(f32[4,24,1024]{2,1,0:T(8,128)} %get-tuple-element.8.tail_ref) | copy-start | bytes 1179652
  33.5 8.7 %copy-start.1 = (f32[8,24,1024]{2,1,0:T(8,128)S(1)}, f32[8,24,1024]{2,1,0:T(8,128)}, u32[]{:S(2)}) copy-start(f32[8,24,1024]{2,1,0:T(8,128)} %get-tuple-element.7.mid_ref) | copy-start | bytes 2359300
  37.6 15.6 %all-to-all-start = ((f32[32,16,128]{2,1,0:T(8,128)}), f32[32,16,128]{2,1,0:T(8,128)S(1)}, u32[]{:S(2)}, u32[]{:S(2)}) async-start(f32[32,16,128]{2,1,0:T(8,128)} %shard_map.87), calls=%async_computation | async-start | bytes 524288 | tf_op jit(solution)/shard_map/all_to_all | solution.py:289
  42.4 11.9 %collective-permute-start.2 = (f32[8,4,1024]{2,1,0:T(4,128)S(1)}, f32[8,4,1024]{2,1,0:T(4,128)S(1)}, u32[]{:S(2)}, u32[]{:S(2)}) collective-permute-start(f32[8,4,1024]{2,1,0:T(4,128)S(1)} %get-tuple-element.12), channel_id=1, source_target_pairs={{0,1},{1,2},{2,3},{3,0},{4,5},{5,6},{6,7},{7,4},{8,9},{9,10},{10,1... | collective-permute-start | bytes 393224 | tf_op jit(solution)/shard_map/ppermute | solution.py:261
  44.2 10.1 %collective-permute-start.3 = (f32[8,4,1024]{2,1,0:T(4,128)S(1)}, f32[8,4,1024]{2,1,0:T(4,128)S(1)}, u32[]{:S(2)}, u32[]{:S(2)}) collective-permute-start(f32[8,4,1024]{2,1,0:T(4,128)S(1)} %get-tuple-element.13), channel_id=1, source_target_pairs={{1,0},{2,1},{3,2},{0,3},{5,4},{6,5},{7,6},{4,7},{9,8},{10,9},{11,1... | collective-permute-start | bytes 393224 | tf_op jit(solution)/shard_map/ppermute | solution.py:262

commit v3 on v2

--- a/solution.py
+++ b/solution.py
@@ -47,12 +47,12 @@
     bound=jnp.where(second,0.5-r4,r4)
     part=cap%128
     lanes=lax.broadcasted_iota(jnp.int32,(16,128),1)
-    zero=jnp.zeros((16,128),jnp.float32)
+    none=jnp.zeros((16,128),jnp.bfloat16)
     def group(g,carry):
         for u in range(UNROLL):
             slot=u%2
             i=g*UNROLL+u
-            acc=[None,None]
+            lefts=[[],[]]; rights=[[],[]]
             for t in range(two//128):
                 def line(k): return rows_ref[k,g,u:u+1,128*t:128*t+128]
                 rx=line(0)
@@ -68,15 +68,18 @@
                 y=jnp.concatenate([jnp.where(my,vy,0.0),jnp.where(my,0.0,vy)],axis=0)
                 mz,vz=taps(2); vz=vz*line(7)
                 z=jnp.concatenate([jnp.where(mz,vz,0.0),jnp.where(mz,0.0,vz)],axis=0)
-                def rows(values,first):
-                    return jnp.concatenate([jnp.concatenate([(values*edge_ref[here,first+4*s+h:first+4*s+h+1,:]).astype(jnp.bfloat16) for h in range(4)],axis=0) for s in range(2)],axis=1)
-                right=rows(y,8)
+                def rows(values,first,dead):
+                    sides=[]
+                    for s in range(2):
+                        sides.append(jnp.concatenate([none if (s,h) in dead else (values*edge_ref[here,first+4*s+h:first+4*s+h+1,:]).astype(jnp.bfloat16) for h in range(4)],axis=0))
+                    return jnp.concatenate(sides,axis=1)
+                right=rows(y,8,[(0,0)])
                 if part and t==cap//128: sides=[(0,jnp.where(lanes<part,z,0.0)),(1,jnp.where(lanes<part,0.0,z))]
                 else: sides=[(int(128*t>=cap),z)]
                 for side,values in sides:
-                    more=lax.dot_general(rows(values,0),right,NT,preferred_element_type=jnp.float32)
-                    acc[side]=more if acc[side] is None else acc[side]+more
+                    lefts[side].append(rows(values,0,[(0,3),(1,0)])); rights[side].append(right)
             base=pl.multiple_of(8*i,8)
+            acc=[lax.dot_general(jnp.concatenate(l,axis=1),jnp.concatenate(r,axis=1),NT,preferred_element_type=jnp.float32) for l,r in zip(lefts,rights)]
             for s in range(2):
                 for h in range(4):
                     line_ref[h,pl.ds(base+8*half*s,16),:]+=acc[s][16*h:16*h+16]
@@ -142,10 +145,17 @@
 
 def amplitude_body(
     place_ref, h_ref, k_ref, l_ref, head_ref, mid_ref, tail_ref, out_ref,
-    phase_ref, shift_ref, along_z_ref, half_ref, wave_ref, *, total_x, total_y
+    phase_ref, shift_ref, along_z_ref, half_ref, wave_ref, grid_ref, sems, *, total_x, total_y
 ):
     rows_x, rows_y, _ = along_z_ref.shape
     depth = mid_ref.shape[2]
+    copies = []
+    start = 0
+    for n, ref in enumerate((head_ref, mid_ref, tail_ref)):
+        target = grid_ref.at[pl.ds(start, ref.shape[0])]
+        copies.append(pltpu.make_async_copy(ref, target, sems.at[n]))
+        copies[-1].start()
+        start += ref.shape[0]
     windows = h_ref.shape[0]
     wide = 16 * windows
 
@@ -173,13 +183,11 @@
     def dot(a, b):
         return jnp.dot(a, b, preferred_element_type=jnp.float32)
 
-    start = 0
-    for ref in (head_ref, mid_ref, tail_ref):
-        count = ref.shape[0]
-        value, rest = split(ref[...].reshape(count * rows_y, depth))
-        found = dot(value, table) + (dot(value, left) + dot(rest, table))
-        along_z_ref[start : start + count] = found.reshape(count, rows_y, 2 * wide)
-        start += count
+    for copy in copies:
+        copy.wait()
+    value, rest = split(grid_ref[...].reshape(rows_x * rows_y, depth))
+    found = dot(value, table) + (dot(value, left) + dot(rest, table))
+    along_z_ref[...] = found.reshape(rows_x, rows_y, 2 * wide)
     row16 = lax.broadcasted_iota(jnp.int32, (16, wide), 0)
     freq_k = centres(k_ref, (16, wide)) + row16 - 8
     now = turn(freq_k, place_ref[1] + 2 * total_y, total_y)
@@ -238,10 +246,11 @@
     windows = miller_h.shape[0]
     wide = 16 * windows
     vmem = pl.BlockSpec(memory_space=pltpu.VMEM)
+    far = pl.BlockSpec(memory_space=pl.ANY)
     smem = pl.BlockSpec(memory_space=pltpu.SMEM)
     return pl.pallas_call(
         functools.partial(amplitude_body, total_x=total_x, total_y=total_y),
-        in_specs=[smem, smem, smem, smem, vmem, vmem, vmem],
+        in_specs=[smem, smem, smem, smem, far, far, far],
         out_specs=vmem,
         out_shape=jax.ShapeDtypeStruct((pieces, 16, 32 * wide // pieces), jnp.float32),
         scratch_shapes=[
@@ -250,8 +259,10 @@
             pltpu.VMEM((rows_x, rows_y, 2 * wide), jnp.float32),
             pltpu.VMEM((rows_x, 32, wide), jnp.float32),
             pltpu.VMEM((512, wide), jnp.float32),
+            pltpu.VMEM((rows_x, rows_y, depth), jnp.float32),
+            pltpu.SemaphoreType.DMA((3,)),
         ],
-        compiler_params=pltpu.CompilerParams(vmem_limit_bytes=40 << 20),
+        compiler_params=pltpu.CompilerParams(vmem_limit_bytes=62 << 20),
         cost_estimate=pl.CostEstimate(flops=5_000_000_000, bytes_accessed=8_000_000, transcendentals=100_000),
     )(place, miller_h, miller_k, miller_l, *grids)
 

time: 55.5 us -> 51.4 us (0.926)
  local copies, waits for them, and re-layouts: 4.07 us -> 0.94 us
  Pallas kernels: 29.3 us -> 27.8 us
    unnamed x14 -> x2, local copies, waits for them, and re-layouts: 3.14 us -> 0.01 us
    pallas_call x1, Pallas kernels: 25.1 us -> 22.4 us  [deposit(): pl.pallas_call(deposit_body, grid=(by,), in_specs=[pl.BlockSpec((1, by, b...]
    pallas_call x1, Pallas kernels: 4.18 us -> 5.43 us  [amplitude(): pl.pallas_call(functools.partial(amplitude_body, total_x=total_x, total_y...]
    another operation x1, other arithmetic: 0.07 us -> 0.65 us  [shards(): jnp.stack([lax.axis_index('gx') * width_x - 4, lax.axis_index('gy') * wid...]
  transfers between devices with their start and end apart: 5 -> 5, of which waited for: 1 -> 1; matrix products, arithmetic and copies ran while one was open for 2% -> 4% of each run, Pallas kernels for 8% -> 11%
where the time goes in v3:
time: 51.4 us; the launch traced here: 51.2 us
  Pallas kernels  27.8 us (54%)
  starting transfers between devices  12 us (23%)
  waiting for transfers between devices  7.9 us (15%)
  other arithmetic  1.78 us (3%)
  local copies, waits for them, and re-layouts  0.94 us (2%)
  between operations  0.72 us (1%)
    pallas_call x1, Pallas kernels, deposit(): pl.pallas_call(deposit_body, grid=(by,), in_specs=[pl.BlockSpec((1, by, b...  22.4 us
    all_to_all x1, waiting for transfers between devices, shards(): received = lax.all_to_all(waves, ('gx', 'gy'), 0, 0, tiled=False)  7.89 us
    pallas_call x1, Pallas kernels, amplitude(): pl.pallas_call(functools.partial(amplitude_body, total_x=total_x, total_y...  5.43 us
    ppermute x2, starting transfers between devices, exchange(): lax.ppermute(head, axis, [((i + 1) % count, i) for i in range(count)])  5.19 us
    all_to_all x1, starting transfers between devices, shards(): received = lax.all_to_all(waves, ('gx', 'gy'), 0, 0, tiled=False)  4.56 us
    ppermute x2, starting transfers between devices, exchange(): lax.ppermute(tail, axis, [(i, (i + 1) % count) for i in range(count)])  2.27 us
  transfers between devices with their start and end apart: 5, of which 1 were waited for; matrix products, arithmetic and copies ran while one was open for 4% of the time, Pallas kernels for 11%

profile of v3, /device:TPU:0, one launch (start us, length us, event | category | flops | bytes accessed | tf_op | source)
XLA Modules:
  0.0 51.2 jit_solution(10509719237612086580)
XLA Ops:
  0.6 22.4 %shard_map.86 = (f32[4,24,1024]{2,1,0:T(8,128)}, f32[8,24,1024]{2,1,0:T(8,128)}, f32[4,24,1024]{2,1,0:T(8,128)}) custom-call(s32[1,2,128]{2,1,0:T(2,128)} %count_ref.1, s32[3,1,2,576,128]{4,3,2,1,0:T(8,128)} %bitcast.7, f32[3,1,2,576,128]{4,3,2,1,0:T(8,128)} %bitcast.8, f32[1,2,576,128]{3,2,1,0:T(8,128)} %bitcast.9), custom_call_target="tpu_custom_call" | custom-call | tf_op jit(solution)/shard_map/pallas_call | solution.py:110
  23.0 0.5 collective-permute-start
  23.4 4.0 %collective-permute-start.1 = (f32[4,24,1024]{2,1,0:T(8,128)}, f32[4,24,1024]{2,1,0:T(8,128)S(1)}, u32[]{:S(2)}, u32[]{:S(2)}) collective-permute-start(f32[4,24,1024]{2,1,0:T(8,128)} %get-tuple-element.9.head_ref), channel_id=1, source_target_pairs={{4,0},{8,4},{12,8},{16,12},{20,16},{24,20},{28,24},{0,28},{5,1},{9... | collective-permute-start | bytes 1179656 | tf_op jit(solution)/shard_map/ppermute | solution.py:273
  27.5 0.6 %pad_add_fusion.1.place_ref = s32[2]{0:T(128)} fusion(s32[1]{0:T(128)} %bitcast.4, s32[1]{0:T(128)} %bitcast.3), kind=kLoop, calls=%fused_computation.5 | loop fusion | flops 2 | bytes 16 | tf_op jit(solution)/shard_map/stack | solution.py:291
  28.1 0.0 copy-start
  28.1 5.4 %shard_map.87 = f32[32,16,128]{2,1,0:T(8,128)} custom-call(s32[2]{0:T(128)} %pad_add_fusion.1.place_ref, s32[8]{0:T(128)} %h_ref.1, s32[8]{0:T(128)} %k_ref.1, s32[8]{0:T(128)} %l_ref.1, f32[4,24,1024]{2,1,0:T(8,128)} %get-tuple-element.9.head_ref, f32[8,24,1024]{2,1,0:T(8,128)} %get-tuple-element.7.mid_ref, f32[4,24,1024]{2,1,0:T(8,128)} %get-tuple-element.8.tail_ref), custom_call_target="tpu_custom_call" | custom-call | flops 5000000000 | bytes 8000000 | tf_op jit(solution)/shard_map/pallas_call | solution.py:251
  33.6 4.6 %all-to-all-start = ((f32[32,16,128]{2,1,0:T(8,128)}), f32[32,16,128]{2,1,0:T(8,128)S(1)}, u32[]{:S(2)}, u32[]{:S(2)}) async-start(f32[32,16,128]{2,1,0:T(8,128)} %shard_map.87), calls=%async_computation | async-start | bytes 524288 | tf_op jit(solution)/shard_map/all_to_all | solution.py:300
  38.1 0.0 collective-permute-done
  38.1 0.0 collective-permute-done.1
  38.2 0.0 copy-done
  38.2 0.1 pad_add_fusion
  38.3 0.1 fusion.2
  38.3 1.8 %collective-permute-start.2 = (f32[8,4,1024]{2,1,0:T(4,128)S(1)}, f32[8,4,1024]{2,1,0:T(4,128)S(1)}, u32[]{:S(2)}, u32[]{:S(2)}) collective-permute-start(f32[8,4,1024]{2,1,0:T(4,128)S(1)} %get-tuple-element.12), channel_id=1, source_target_pairs={{0,1},{1,2},{2,3},{3,0},{4,5},{5,6},{6,7},{7,4},{8,9},{9,10},{10,1... | collective-permute-start | bytes 393224 | tf_op jit(solution)/shard_map/ppermute | solution.py:272
  40.1 1.2 %collective-permute-start.3 = (f32[8,4,1024]{2,1,0:T(4,128)S(1)}, f32[8,4,1024]{2,1,0:T(4,128)S(1)}, u32[]{:S(2)}, u32[]{:S(2)}) collective-permute-start(f32[8,4,1024]{2,1,0:T(4,128)S(1)} %get-tuple-element.13), channel_id=1, source_target_pairs={{1,0},{2,1},{3,2},{0,3},{5,4},{6,5},{7,6},{4,7},{9,8},{10,9},{11,1... | collective-permute-start | bytes 393224 | tf_op jit(solution)/shard_map/ppermute | solution.py:273
  41.3 7.9 %all-to-all-done = f32[32,16,128]{2,1,0:T(8,128)S(1)} async-done(((f32[32,16,128]{2,1,0:T(8,128)}), f32[32,16,128]{2,1,0:T(8,128)S(1)}, u32[]{:S(2)}, u32[]{:S(2)}) %all-to-all-start) | async-done | bytes 262176 | tf_op jit(solution)/shard_map/all_to_all | solution.py:300
  49.2 0.1 mul.15
  49.4 0.1 reduce_sum.19
  49.5 0.1 copy.10
  49.6 0.7 %reshape.9 = f32[4,256]{1,0:T(4,128)} reshape(f32[4,16,16]{2,1,0:T(8,128)S(1)} %copy.10) | data formatting | bytes 8192 | tf_op jit(solution)/shard_map/reshape | solution.py:304
  50.3 0.0 collective-permute-done.2
  50.3 0.0 collective-permute-done.3
  50.3 0.9 %fusion = f32[8,16,1024]{2,1,0:T(8,128)} fusion(f32[8,24,1024]{2,1,0:T(8,128)S(1)} %pad_add_fusion, f32[8,4,1024]{2,1,0:T(4,128)S(1)} %collective-permute-done.3, f32[8,4,1024]{2,1,0:T(4,128)S(1)} %collective-permute-done.2), kind=kLoop, calls=%fused_computation.2 | loop fusion | flops 262144 | bytes 1310720 | tf_op jit(solution)/shard_map/add | solution.py:283
  (3 shorter events, 0.0 us)
Async XLA Ops:
  23.0 15.1 %collective-permute-start = (f32[4,24,1024]{2,1,0:T(8,128)}, f32[4,24,1024]{2,1,0:T(8,128)S(1)}, u32[]{:S(2)}, u32[]{:S(2)}) collective-permute-start(f32[4,24,1024]{2,1,0:T(8,128)} %get-tuple-element.8.tail_ref), channel_id=1, source_target_pairs={{0,4},{4,8},{8,12},{12,16},{16,20},{20,24},{24,28},{28,0},{1,5},{5... | collective-permute-start | bytes 1179656 | tf_op jit(solution)/shard_map/ppermute | solution.py:272
  23.4 14.7 %collective-permute-start.1 = (f32[4,24,1024]{2,1,0:T(8,128)}, f32[4,24,1024]{2,1,0:T(8,128)S(1)}, u32[]{:S(2)}, u32[]{:S(2)}) collective-permute-start(f32[4,24,1024]{2,1,0:T(8,128)} %get-tuple-element.9.head_ref), channel_id=1, source_target_pairs={{4,0},{8,4},{12,8},{16,12},{20,16},{24,20},{28,24},{0,28},{5,1},{9... | collective-permute-start | bytes 1179656 | tf_op jit(solution)/shard_map/ppermute | solution.py:273
  28.1 10.0 %copy-start = (f32[8,24,1024]{2,1,0:T(8,128)S(1)}, f32[8,24,1024]{2,1,0:T(8,128)}, u32[]{:S(2)}) copy-start(f32[8,24,1024]{2,1,0:T(8,128)} %get-tuple-element.7.mid_ref) | copy-start | bytes 2359300
  33.6 15.6 %all-to-all-start = ((f32[32,16,128]{2,1,0:T(8,128)}), f32[32,16,128]{2,1,0:T(8,128)S(1)}, u32[]{:S(2)}, u32[]{:S(2)}) async-start(f32[32,16,128]{2,1,0:T(8,128)} %shard_map.87), calls=%async_computation | async-start | bytes 524288 | tf_op jit(solution)/shard_map/all_to_all | solution.py:300
  38.3 11.9 %collective-permute-start.2 = (f32[8,4,1024]{2,1,0:T(4,128)S(1)}, f32[8,4,1024]{2,1,0:T(4,128)S(1)}, u32[]{:S(2)}, u32[]{:S(2)}) collective-permute-start(f32[8,4,1024]{2,1,0:T(4,128)S(1)} %get-tuple-element.12), channel_id=1, source_target_pairs={{0,1},{1,2},{2,3},{3,0},{4,5},{5,6},{6,7},{7,4},{8,9},{9,10},{10,1... | collective-permute-start | bytes 393224 | tf_op jit(solution)/shard_map/ppermute | solution.py:272
  40.1 10.1 %collective-permute-start.3 = (f32[8,4,1024]{2,1,0:T(4,128)S(1)}, f32[8,4,1024]{2,1,0:T(4,128)S(1)}, u32[]{:S(2)}, u32[]{:S(2)}) collective-permute-start(f32[8,4,1024]{2,1,0:T(4,128)S(1)} %get-tuple-element.13), channel_id=1, source_target_pairs={{1,0},{2,1},{3,2},{0,3},{5,4},{6,5},{7,6},{4,7},{9,8},{10,9},{11,1... | collective-permute-start | bytes 393224 | tf_op jit(solution)/shard_map/ppermute | solution.py:273

commit v4 on v1

v4 whole, which is shorter than its diff:
```python
import functools
import math

import jax
import jax.numpy as jnp
from jax import lax
from jax.experimental import pallas as pl
from jax.experimental.pallas import tpu as pltpu
from jax.sharding import PartitionSpec as P

KERNEL_SIGMA = 0.9
NORMAL = 1.0 / (KERNEL_SIGMA * math.sqrt(2.0 * math.pi))
SCALE = math.sqrt(0.5 / math.log(2.0)) / KERNEL_SIGMA
LOG_NORMAL = math.log2(NORMAL)
FAR = -1.0e4
LANES_BY_LANES = (((1,), (1,)), ((), ()))
UNROLL = 32
FINE = 32


def turn(freqs, place, extent):
    product = freqs * place
    if extent & (extent - 1) == 0:
        product = product & (extent - 1)
    else:
        product = lax.rem(lax.rem(product, extent) + extent, extent)
    if extent & (extent - 1) or extent < 8:
        angle = product.astype(jnp.float32) * (2.0 * math.pi / extent)
        return jnp.cos(angle), jnp.sin(angle)
    quarters = (product + extent // 8) >> ((extent // 4).bit_length() - 1)
    angle = (product - quarters * (extent // 4)).astype(jnp.float32) * (2.0 * math.pi / extent)
    square = angle * angle
    cos = jnp.full_like(angle, -1.0 / math.factorial(10))
    for n in (8, 6, 4, 2, 0):
        cos = cos * square + (-1.0) ** (n // 2) / math.factorial(n)
    sin = jnp.full_like(angle, 1.0 / math.factorial(9))
    for n in (7, 5, 3, 1):
        sin = sin * square + (-1.0) ** (n // 2) / math.factorial(n)
    sin = sin * angle
    odd = (quarters & 1) == 1
    cos, sin = jnp.where(odd, sin, cos), jnp.where(odd, cos, sin)
    cos = jnp.where(((quarters + 1) & 2) == 2, -cos, cos)
    return cos, jnp.where((quarters & 2) == 2, -sin, sin)


def times(one, other):
    return (
        one[0] * other[0] - one[1] * other[1],
        one[0] * other[1] + one[1] * other[0],
    )


def split(value):
    head = value.astype(jnp.bfloat16)
    return head, (value - head.astype(jnp.float32)).astype(jnp.bfloat16)


def phase_tables(place, millers, extents, shift_ref, table_ref, phase_y_ref, phase_x_ref):
    h_ref, k_ref, l_ref = millers
    total_x, total_y, depth = extents
    windows = h_ref.shape[0]
    wide = 16 * windows

    def centres(ref, rows):
        window = lax.broadcasted_iota(jnp.int32, (rows, wide), 1) // 16
        found = jnp.zeros((rows, wide), jnp.int32)
        for w in range(windows):
            found = jnp.where(window == w, ref[w], found)
        return found - 8

    lane = lax.broadcasted_iota(jnp.int32, (FINE, wide), 1) % 16
    below = lax.broadcasted_iota(jnp.int32, (FINE, wide), 0)
    freq_l = centres(l_ref, FINE) + lane
    fine = turn(freq_l, below, depth)
    coarse = turn(freq_l, below * FINE, depth)
    shift_ref[0] = coarse[0]
    shift_ref[1] = coarse[1]
    for step in range(depth // FINE):
        now = times(fine, (shift_ref[0, step : step + 1], shift_ref[1, step : step + 1]))
        at = pl.ds(step * FINE, FINE)
        for side, value in ((0, now[0]), (1, -now[1])):
            head, rest = split(value)
            table_ref[0, at, side * wide : (side + 1) * wide] = head
            table_ref[1, at, side * wide : (side + 1) * wide] = rest
    row = lax.broadcasted_iota(jnp.int32, (16, wide), 0)
    for ref, out_ref, start, total in (
        (k_ref, phase_y_ref, place[1], total_y),
        (h_ref, phase_x_ref, place[0], total_x),
    ):
        freqs = centres(ref, 16) + row
        now = turn(freqs, start + 2 * total, total)
        step = turn(freqs, 1, total)
        for n in range(out_ref.shape[0]):
            out_ref[n, 0:16] = now[0]
            out_ref[n, 16:32] = now[1]
            now = times(now, step)


def transforms(grid_ref, table_ref, phase_y_ref, phase_x_ref, along_z_ref, half_ref, wave_ref, out_ref, late):
    rows_x, rows_y, depth = grid_ref.shape
    wide = wave_ref.shape[1]

    def dot(a, b):
        return jnp.dot(a, b, preferred_element_type=jnp.float32)

    value, rest = split(grid_ref[...].reshape(rows_x * rows_y, depth))
    found = dot(value, table_ref[0]) + (dot(value, table_ref[1]) + dot(rest, table_ref[0]))
    along_z_ref[...] = found.reshape(rows_x, rows_y, 2 * wide)
    for copy in late:
        copy.wait()
    group = 5 if rows_x % 5 == 0 else 1
    for x in range(0, rows_x, group):
        real = [jnp.zeros((16, wide), jnp.float32)] * group
        imag = [jnp.zeros((16, wide), jnp.float32)] * group
        for y in range(1, rows_y):
            cos = phase_y_ref[y, 0:16]
            sin = phase_y_ref[y, 16:32]
            for g in range(group):
                a = along_z_ref[x + g, y : y + 1, 0:wide]
                b = along_z_ref[x + g, y : y + 1, wide : 2 * wide]
                real[g] = real[g] + (a * cos + b * sin)
                imag[g] = imag[g] + (b * cos - a * sin)
        for g in range(group):
            half_ref[x + g, 0:16] = real[g]
            half_ref[x + g, 16:32] = imag[g]
    group = 4
    for h in range(0, 16, group):
        real = [jnp.zeros((16, wide), jnp.float32)] * group
        imag = [jnp.zeros((16, wide), jnp.float32)] * group
        for x in range(rows_x):
            a = half_ref[x, 0:16]
            b = half_ref[x, 16:32]
            for g in range(group):
                cos = phase_x_ref[x, h + g : h + g + 1]
                sin = phase_x_ref[x, 16 + h + g : 17 + h + g]
                real[g] = real[g] + (a * cos + b * sin)
                imag[g] = imag[g] + (b * cos - a * sin)
        for g in range(group):
            wave_ref[pl.ds(32 * (h + g), 16)] = real[g]
            wave_ref[pl.ds(32 * (h + g) + 16, 16)] = imag[g]
    turned = jnp.transpose(wave_ref[...])
    pieces, _, lanes = out_ref.shape
    per_window = pieces // (wide // 16)
    for piece in range(pieces):
        w, part = piece // per_window, piece % per_window
        out_ref[piece] = turned[16 * w : 16 * w + 16, part * lanes : (part + 1) * lanes]


def deposit_column(column, fetches, next_fetches, cell_ref, frac_ref, weight_ref, count_ref, rows_ref, edge_ref, line_ref):
    cap, blocks_z = weight_ref.shape
    depth = 8 * blocks_z
    half = blocks_z // 2
    two = 2 * cap

    def paired(value):
        value = jnp.transpose(value)
        return jnp.concatenate([value[:half], value[half:]], axis=1).reshape(half // UNROLL, UNROLL, two)

    line_ref[...] = jnp.zeros_like(line_ref)
    for d in range(3):
        fetches[2 * d].wait()
        fetches[2 * d + 1].wait()
        cell = cell_ref[d].astype(jnp.float32)
        place = cell + frac_ref[d]
        if d == 0:
            upper = jnp.where(cell > 3.5, 1.0, 0.0)
            rows_ref[0] = paired((place - 3.5) * SCALE)
            rows_ref[1] = paired(upper)
            rows_ref[2] = paired(cell - 4.0 * upper)
        else:
            rows_ref[2 * d + 1] = paired(place * SCALE)
            rows_ref[2 * d + 2] = paired(cell)
    fetches[6].wait()
    slots = lax.broadcasted_iota(jnp.int32, (cap, blocks_z), 0)
    rows_ref[7] = paired(jnp.where(slots < count_ref[0, pl.ds(column, 1), :], weight_ref[...], 0.0))
    next_fetches()
    row = lax.broadcasted_iota(jnp.int32, (8, 128), 0)
    row8 = row.astype(jnp.float32)
    low = (row8 - 4.0) * SCALE
    high = (row8 + 4.0) * SCALE
    row4 = (row % 4).astype(jnp.float32)
    second = row >= 4
    nodes = (4.0 * row4 - 6.0) * SCALE
    first = jnp.where(second, 1.0, 0.0)
    on_lower = jnp.where((row4 >= first) & (row4 <= first + 1.0), 0.0, FAR)
    on_upper = jnp.where((row4 >= first + 1.0) & (row4 <= first + 2.0), 0.0, FAR)
    slopes = (row4 - 1.5) * (2.0 * SCALE)
    sign = jnp.where(second, -1.0, 1.0)
    bound = jnp.where(second, 0.5 - row4, row4)
    part = cap % 128
    lanes = lax.broadcasted_iota(jnp.int32, (16, 128), 1)
    none = jnp.zeros((16, 128), jnp.bfloat16)

    def group(g, carry):
        for u in range(UNROLL):
            lefts = [[], []]
            rights = [[], []]
            for t in range(two // 128):

                def line(k):
                    return rows_ref[k, g, u : u + 1, 128 * t : 128 * t + 128]

                def taps(d):
                    inside = row8 > line(2 * d + 2)
                    away = jnp.where(inside, low, high) - line(2 * d + 1)
                    return inside, jnp.exp2(LOG_NORMAL - away * away)

                def halves(inside, value):
                    return jnp.concatenate([jnp.where(inside, value, 0.0), jnp.where(inside, 0.0, value)], axis=0)

                here = (u % 2) * (two // 128) + t
                place = line(0)
                away = place - nodes
                edge_ref[here, 0:8] = jnp.exp2(jnp.where(line(1) > 0.5, on_upper, on_lower) - away * away)
                edge_ref[here, 8:16] = jnp.exp2(jnp.where(bound > sign * line(2), slopes * place, FAR))
                inside, value = taps(1)
                taps_y = halves(inside, value)
                inside, value = taps(2)
                scaled = halves(inside, value * line(7))

                def rows(values, start, dead):
                    sides = []
                    for s in range(2):
                        sides.append(
                            jnp.concatenate(
                                [
                                    none
                                    if (s, n) in dead
                                    else (
                                        values * edge_ref[here, start + 4 * s + n : start + 4 * s + n + 1, :]
                                    ).astype(jnp.bfloat16)
                                    for n in range(4)
                                ],
                                axis=0,
                            )
                        )
                    return jnp.concatenate(sides, axis=1)

                right = rows(taps_y, 8, [(0, 0)])
                if part and t == cap // 128:
                    owned = [(0, jnp.where(lanes < part, scaled, 0.0)), (1, jnp.where(lanes < part, 0.0, scaled))]
                else:
                    owned = [(int(128 * t >= cap), scaled)]
                for side, values in owned:
                    lefts[side].append(rows(values, 0, [(0, 3), (1, 0)]))
                    rights[side].append(right)
            base = pl.multiple_of(8 * (g * UNROLL + u), 8)
            for s in range(2):
                found = lax.dot_general(
                    jnp.concatenate(lefts[s], axis=1),
                    jnp.concatenate(rights[s], axis=1),
                    LANES_BY_LANES,
                    preferred_element_type=jnp.float32,
                )
                for n in range(4):
                    line_ref[n, pl.ds(base + 8 * half * s, 16), :] += found[16 * n : 16 * n + 16]
        return carry

    lax.fori_loop(0, half // UNROLL, group, 0)


def add_column(column, line_ref, grid_ref, finished):
    depth = grid_ref.shape[2]
    for n in range(4):
        line_ref[n, 4:8, :] += line_ref[n, depth + 4 : depth + 8, :]
        line_ref[n, depth : depth + 4, :] += line_ref[n, 0:4, :]
    at = pl.ds(pl.multiple_of(8 * column, 8), 16)
    for n in range(4):
        for c in range(depth // 128):
            turned = jnp.transpose(line_ref[n, 128 * c + 4 : 128 * c + 132, :])
            for k in range(4):
                near = k - 1.5
                factor = NORMAL * math.exp((-near * (4 * n - 6) - 0.5 * near * near) / KERNEL_SIGMA**2)
                grid_ref[4 * n + k, at, 128 * c : 128 * c + 128] += turned[16 * k : 16 * k + 16] * factor
        finished(n)


def deposit_body(
    h_ref, k_ref, l_ref, count_ref, cell_ref, frac_ref, weight_ref,
    head_ref, mid_ref, tail_ref, table_out_ref, phase_y_out_ref, phase_x_out_ref,
    cells_ref, fracs_ref, weights_ref, rows_ref, edge_ref, line_ref, grid_ref, shift_ref,
    table_ref, phase_y_ref, phase_x_ref, in_sems, out_sems, *, totals,
):
    columns = weights_ref.shape[0]
    rows_x, rows_y, depth = grid_ref.shape

    def fetches(j):
        found = []
        for d in range(3):
            found.append(pltpu.make_async_copy(cell_ref.at[d, 0, j], cells_ref.at[j, d], in_sems.at[j, 2 * d]))
            found.append(pltpu.make_async_copy(frac_ref.at[d, 0, j], fracs_ref.at[j, d], in_sems.at[j, 2 * d + 1]))
        found.append(pltpu.make_async_copy(weight_ref.at[0, j], weights_ref.at[j], in_sems.at[j, 6]))
        return found

    for copy in fetches(0):
        copy.start()
    place = (lax.axis_index("gx") * (rows_x - 8) - 3, lax.axis_index("gy") * (rows_y - 8) - 4)
    phase_tables(
        place, (h_ref, k_ref, l_ref), (*totals, depth), shift_ref, table_ref, phase_y_ref, phase_x_ref
    )
    leaving = [
        pltpu.make_async_copy(table_ref, table_out_ref, out_sems.at[0]),
        pltpu.make_async_copy(phase_y_ref, phase_y_out_ref, out_sems.at[1]),
        pltpu.make_async_copy(phase_x_ref, phase_x_out_ref, out_sems.at[2]),
    ]
    for copy in leaving:
        copy.start()
    grid_ref[...] = jnp.zeros_like(grid_ref)

    def column(j, carry):
        def next_fetches():
            @pl.when(j < columns - 1)
            def _():
                for copy in fetches(j + 1):
                    copy.start()

        deposit_column(
            j, fetches(j), next_fetches, cells_ref.at[j], fracs_ref.at[j], weights_ref.at[j], count_ref, rows_ref, edge_ref, line_ref
        )

        @pl.when(j < columns - 1)
        def _():
            add_column(j, line_ref, grid_ref, lambda n: None)

        return carry

    lax.fori_loop(0, columns, column, 0)

    def finished(n):
        if n != 1:
            face, start = {0: (head_ref, 1), 2: (mid_ref, 4), 3: (tail_ref, 12)}[n]
            copy = pltpu.make_async_copy(
                grid_ref.at[pl.ds(start, face.shape[0])], face, out_sems.at[len(leaving)]
            )
            copy.start()
            leaving.append(copy)

    add_column(columns - 1, line_ref, grid_ref, finished)
    for copy in leaving:
        copy.wait()


def transform_body(
    head_ref, mid_ref, tail_ref, table_in_ref, phase_y_in_ref, phase_x_in_ref, out_ref,
    grid_ref, table_ref, phase_y_ref, phase_x_ref, along_z_ref, half_ref, wave_ref, sems,
):
    faces = []
    start = 0
    for n, ref in enumerate((head_ref, mid_ref, tail_ref)):
        faces.append(pltpu.make_async_copy(ref, grid_ref.at[pl.ds(start, ref.shape[0])], sems.at[n]))
        start += ref.shape[0]
    tables = [
        pltpu.make_async_copy(table_in_ref, table_ref, sems.at[3]),
        pltpu.make_async_copy(phase_y_in_ref, phase_y_ref, sems.at[4]),
        pltpu.make_async_copy(phase_x_in_ref, phase_x_ref, sems.at[5]),
    ]
    tables[0].start()
    for copy in faces:
        copy.start()
    for copy in tables[1:]:
        copy.start()
    tables[0].wait()
    for copy in faces:
        copy.wait()
    transforms(grid_ref, table_ref, phase_y_ref, phase_x_ref, along_z_ref, half_ref, wave_ref, out_ref, tables[1:])


FAR_AWAY = pl.BlockSpec(memory_space=pl.ANY)
NEARBY = pl.BlockSpec(memory_space=pltpu.VMEM)


def deposit(cell, frac, weight, count, miller_h, miller_k, miller_l, totals):
    _, columns, blocks_z, cap = weight.shape
    depth = 8 * blocks_z
    rows_x, rows_y = 16, 8 * columns + 8
    wide = 16 * miller_h.shape[0]

    def turned(value):
        return jnp.swapaxes(value, -1, -2)

    smem = pl.BlockSpec(memory_space=pltpu.SMEM)
    f32 = jnp.float32
    tables = [((2, depth, 2 * wide), jnp.bfloat16), ((rows_y, 32, wide), f32), ((rows_x - 1, 32, wide), f32)]
    return pl.pallas_call(
        functools.partial(deposit_body, totals=totals),
        in_specs=[smem, smem, smem, NEARBY, FAR_AWAY, FAR_AWAY, FAR_AWAY],
        out_specs=[FAR_AWAY] * 6,
        out_shape=[jax.ShapeDtypeStruct((n, rows_y, depth), f32) for n in (3, 8, 4)]
        + [jax.ShapeDtypeStruct(*table) for table in tables],
        scratch_shapes=[
            pltpu.VMEM((columns, 3, cap, blocks_z), jnp.int32),
            pltpu.VMEM((columns, 3, cap, blocks_z), f32),
            pltpu.VMEM((columns, cap, blocks_z), f32),
            pltpu.VMEM((8, blocks_z // 2 // UNROLL, UNROLL, 2 * cap), f32),
            pltpu.VMEM((2 * (2 * cap // 128), 16, 128), f32),
            pltpu.VMEM((4, depth + 8, 64), f32),
            pltpu.VMEM((rows_x, rows_y, depth), f32),
            pltpu.VMEM((2, depth // FINE, wide), f32),
            *[pltpu.VMEM(*table) for table in tables],
            pltpu.SemaphoreType.DMA((columns, 7)),
            pltpu.SemaphoreType.DMA((6,)),
        ],
        compiler_params=pltpu.CompilerParams(vmem_limit_bytes=60 << 20),
    )(miller_h, miller_k, miller_l, count, turned(cell), turned(frac), turned(weight))


def transform(faces, tables, pieces):
    _, rows_y, depth = faces[0].shape
    rows_x = sum(face.shape[0] for face in faces)
    wide = tables[1].shape[2]
    f32 = jnp.float32
    return pl.pallas_call(
        transform_body,
        in_specs=[FAR_AWAY] * 6,
        out_specs=NEARBY,
        out_shape=jax.ShapeDtypeStruct((pieces, 16, 32 * wide // pieces), f32),
        scratch_shapes=[
            pltpu.VMEM((rows_x, rows_y, depth), f32),
            *[pltpu.VMEM(table.shape, table.dtype) for table in tables],
            pltpu.VMEM((rows_x, rows_y, 2 * wide), f32),
            pltpu.VMEM((rows_x, 32, wide), f32),
            pltpu.VMEM((512, wide), f32),
            pltpu.SemaphoreType.DMA((6,)),
        ],
        compiler_params=pltpu.CompilerParams(vmem_limit_bytes=60 << 20),
        cost_estimate=pl.CostEstimate(flops=5_000_000_000, bytes_accessed=8_000_000, transcendentals=0),
    )(*faces, *tables)


def exchange(head, tail, axis):
    count = lax.axis_size(axis)
    before = lax.ppermute(tail, axis, [(i, (i + 1) % count) for i in range(count)])
    after = lax.ppermute(head, axis, [((i + 1) % count, i) for i in range(count)])
    return before, after


def added(inner, before, after, dim):
    length = inner.shape[dim]
    widths = [(0, 0)] * inner.ndim
    widths[dim] = (0, length - before.shape[dim])
    leading = jnp.pad(before, widths)
    widths[dim] = (length - after.shape[dim], 0)
    return inner + leading + jnp.pad(after, widths)


def shards(atom_cell, atom_frac, atom_weight, block_count, miller_h, miller_k, miller_l):
    blocks_x, blocks_y, blocks_z, _ = atom_weight.shape
    count_x, count_y = lax.axis_size("gx"), lax.axis_size("gy")
    width_x, width_y, depth = 8 * blocks_x, 8 * blocks_y, 8 * blocks_z
    total_x, total_y = width_x * count_x, width_y * count_y
    pieces = count_x * count_y
    head, mid, tail, *tables = deposit(
        atom_cell, atom_frac, atom_weight, block_count, miller_h, miller_k, miller_l, (total_x, total_y)
    )
    before, after = exchange(head, tail, "gx")
    waves = transform((head, mid, tail), tables, pieces)
    before, after, _ = lax.optimization_barrier((before, after, waves))
    received = lax.all_to_all(waves, ("gx", "gy"), 0, 0, tiled=False)
    rows = miller_h.shape[0] * 16 // pieces
    summed = jnp.sum(received, axis=0).reshape(16, rows, 2, 16)
    power = jnp.sum(summed * summed, axis=2) / float(total_x * total_y * depth)
    intensity = jnp.transpose(power, (1, 2, 0)).reshape(rows, 256)
    wide = added(mid, before, after, 0)
    before, after = exchange(wide[:, :4], wide[:, width_y + 4 :], "gy")
    density = added(wide[:, 4 : width_y + 4], before, after, 1)
    return (density, intensity)


def solution(mesh):
    in_specs = (
        P(None, "gx", "gy", None, None),
        P(None, "gx", "gy", None, None),
        P("gx", "gy", None, None),
        P("gx", "gy", None),
        P(),
        P(),
        P(),
    )
    out_specs = (P("gx", "gy", None), P(("gx", "gy"), None))
    return jax.shard_map(shards, mesh=mesh, in_specs=in_specs, out_specs=out_specs, check_vma=False)
```

time: 82.8 us -> 50.8 us (0.61)
  Pallas kernels: 41.1 us -> 26.6 us
  waiting for transfers between devices: 21.9 us -> 7.89 us
  local copies, waits for them, and re-layouts: 9.43 us -> 0.94 us
  starting transfers between devices: 7.9 us -> 13.3 us
    pallas_call x2, Pallas kernels: 41.1 us -> 26.6 us  [the longest x1 22 us: deposit(): pl.pallas_call(functools.partial(deposit_body, totals=totals), in_specs=[...]
    ppermute x4, waiting for transfers between devices: 12.9 us -> 0.01 us  [the longest x2 0.01 us: exchange(): lax.ppermute(head, axis, [((i + 1) % count, i) for i in range(count)])]
    unnamed x17 -> x2, local copies, waits for them, and re-layouts: 8.51 us -> 0.01 us
    ppermute x4, starting transfers between devices: 3.26 us -> 7.52 us  [the longest x2 5.7 us: exchange(): lax.ppermute(head, axis, [((i + 1) % count, i) for i in range(count)])]
    all_to_all x1, waiting for transfers between devices: 9.03 us -> 7.88 us  [shards(): received = lax.all_to_all(waves, ('gx', 'gy'), 0, 0, tiled=False)]
    all_to_all x1, starting transfers between devices: 4.64 us -> 5.79 us  [shards(): received = lax.all_to_all(waves, ('gx', 'gy'), 0, 0, tiled=False)]
    concatenate x2 -> x0, other arithmetic: 0.91 us -> none  [with_margins(): return jnp.concatenate(parts, axis=dim)]
  transfers between devices with their start and end apart: 5 -> 5, of which waited for: 3 -> 1; matrix products, arithmetic and copies ran while one was open for 1% -> 2% of each run, Pallas kernels for 5% -> 9%
where the time goes in v4:
time: 50.8 us; the launch traced here: 50.6 us
  Pallas kernels  26.6 us (52%)
  starting transfers between devices  13.3 us (26%)
  waiting for transfers between devices  7.89 us (16%)
  other arithmetic  1.15 us (2%)
  local copies, waits for them, and re-layouts  0.94 us (2%)
  between operations  0.72 us (1%)
    pallas_call x1, Pallas kernels, deposit(): pl.pallas_call(functools.partial(deposit_body, totals=totals), in_specs=[...  22 us
    all_to_all x1, waiting for transfers between devices, shards(): received = lax.all_to_all(waves, ('gx', 'gy'), 0, 0, tiled=False)  7.88 us
    all_to_all x1, starting transfers between devices, shards(): received = lax.all_to_all(waves, ('gx', 'gy'), 0, 0, tiled=False)  5.79 us
    ppermute x2, starting transfers between devices, exchange(): lax.ppermute(head, axis, [((i + 1) % count, i) for i in range(count)])  5.7 us
    pallas_call x1, Pallas kernels, transform(): pl.pallas_call(transform_body, in_specs=[FAR_AWAY] * 6, out_specs=NEARBY,...  4.54 us
    ppermute x2, starting transfers between devices, exchange(): lax.ppermute(tail, axis, [(i, (i + 1) % count) for i in range(count)])  1.82 us
  transfers between devices with their start and end apart: 5, of which 1 were waited for; matrix products, arithmetic and copies ran while one was open for 2% of the time, Pallas kernels for 9%

profile of v4, /device:TPU:0, one launch (start us, length us, event | category | flops | bytes accessed | tf_op | source)
XLA Modules:
  0.0 50.6 jit_solution(14912678338189210664)
XLA Ops:
  0.6 22.0 %shard_map.86 = (f32[3,24,1024]{2,1,0:T(8,128)}, f32[8,24,1024]{2,1,0:T(8,128)}, f32[4,24,1024]{2,1,0:T(8,128)}, bf16[2,1024,256]{2,1,0:T(8,128)(2,1)}, f32[24,32,128]{2,1,0:T(8,128)}, /*index=5*/f32[15,32,128]{2,1,0:T(8,128)}) custom-call(s32[8]{0:T(128)} %h_ref.1, s32[8]{0:T(128)} %k_ref.1, s32[8]{0:T(128)} %l_ref.1, s32[1,2,128]{2,1,0:T(2,128)} %count_ref.1, ...), custom_call_target="tpu_custom_call" | custom-call | tf_op jit(solution)/shard_map/pallas_call | solution.py:384
  22.7 4.5 %collective-permute-start.1 = (f32[3,24,1024]{2,1,0:T(8,128)}, f32[3,24,1024]{2,1,0:T(8,128)S(1)}, u32[]{:S(2)}, u32[]{:S(2)}) collective-permute-start(f32[3,24,1024]{2,1,0:T(8,128)} %get-tuple-element.12.head_ref), channel_id=1, source_target_pairs={{4,0},{8,4},{12,8},{16,12},{20,16},{24,20},{28,24},{0,28},{5,1},{9... | collective-permute-start | bytes 884744 | tf_op jit(solution)/shard_map/ppermute | solution.py:433
  27.2 0.0 collective-permute-start
  27.2 0.0 copy-start
  27.2 4.5 %shard_map.87 = f32[32,16,128]{2,1,0:T(8,128)} custom-call(f32[3,24,1024]{2,1,0:T(8,128)} %get-tuple-element.12.head_ref, f32[8,24,1024]{2,1,0:T(8,128)} %get-tuple-element.10.mid_ref, f32[4,24,1024]{2,1,0:T(8,128)} %get-tuple-element.11.tail_ref, bf16[2,1024,256]{2,1,0:T(8,128)(2,1)} %get-tuple-element.13.table_in_ref, ...), custom_call_target="tpu_custom_call" | custom-call | flops 5000000000 | bytes 8000000 | tf_op jit(solution)/shard_map/pallas_call | solution.py:412
  31.8 5.8 %all-to-all-start = ((f32[32,16,128]{2,1,0:T(8,128)}), f32[32,16,128]{2,1,0:T(8,128)S(1)}, u32[]{:S(2)}, u32[]{:S(2)}) async-start(f32[32,16,128]{2,1,0:T(8,128)} %shard_map.87), calls=%async_computation | async-start | bytes 524288 | tf_op jit(solution)/shard_map/all_to_all | solution.py:458
  37.6 0.0 collective-permute-done.1
  37.6 0.0 collective-permute-done
  37.6 0.0 copy-done
  37.6 0.1 pad_add_fusion
  37.7 0.1 fusion.2
  37.8 1.8 %collective-permute-start.2 = (f32[8,4,1024]{2,1,0:T(4,128)S(1)}, f32[8,4,1024]{2,1,0:T(4,128)S(1)}, u32[]{:S(2)}, u32[]{:S(2)}) collective-permute-start(f32[8,4,1024]{2,1,0:T(4,128)S(1)} %get-tuple-element.18), channel_id=1, source_target_pairs={{0,1},{1,2},{2,3},{3,0},{4,5},{5,6},{6,7},{7,4},{8,9},{9,10},{10,1... | collective-permute-start | bytes 393224 | tf_op jit(solution)/shard_map/ppermute | solution.py:432
  39.6 1.2 %collective-permute-start.3 = (f32[8,4,1024]{2,1,0:T(4,128)S(1)}, f32[8,4,1024]{2,1,0:T(4,128)S(1)}, u32[]{:S(2)}, u32[]{:S(2)}) collective-permute-start(f32[8,4,1024]{2,1,0:T(4,128)S(1)} %get-tuple-element.19), channel_id=1, source_target_pairs={{1,0},{2,1},{3,2},{0,3},{5,4},{6,5},{7,6},{4,7},{9,8},{10,9},{11,1... | collective-permute-start | bytes 393224 | tf_op jit(solution)/shard_map/ppermute | solution.py:433
  40.7 7.9 %all-to-all-done = f32[32,16,128]{2,1,0:T(8,128)S(1)} async-done(((f32[32,16,128]{2,1,0:T(8,128)}), f32[32,16,128]{2,1,0:T(8,128)S(1)}, u32[]{:S(2)}, u32[]{:S(2)}) %all-to-all-start) | async-done | bytes 262176 | tf_op jit(solution)/shard_map/all_to_all | solution.py:458
  48.7 0.1 mul.7
  48.8 0.1 reduce_sum.19
  48.9 0.1 copy.10
  49.0 0.7 %reshape.9 = f32[4,256]{1,0:T(4,128)} reshape(f32[4,16,16]{2,1,0:T(8,128)S(1)} %copy.10) | data formatting | bytes 8192 | tf_op jit(solution)/shard_map/reshape | solution.py:462
  49.7 0.0 collective-permute-done.2
  49.7 0.0 collective-permute-done.3
  49.7 0.9 %fusion = f32[8,16,1024]{2,1,0:T(8,128)} fusion(f32[8,24,1024]{2,1,0:T(8,128)S(1)} %pad_add_fusion, f32[8,4,1024]{2,1,0:T(4,128)S(1)} %collective-permute-done.3, f32[8,4,1024]{2,1,0:T(4,128)S(1)} %collective-permute-done.2), kind=kLoop, calls=%fused_computation.2 | loop fusion | flops 262144 | bytes 1310720 | tf_op jit(solution)/shard_map/add | solution.py:443
  (3 shorter events, 0.0 us)
Async XLA Ops:
  22.7 14.9 %collective-permute-start.1 = (f32[3,24,1024]{2,1,0:T(8,128)}, f32[3,24,1024]{2,1,0:T(8,128)S(1)}, u32[]{:S(2)}, u32[]{:S(2)}) collective-permute-start(f32[3,24,1024]{2,1,0:T(8,128)} %get-tuple-element.12.head_ref), channel_id=1, source_target_pairs={{4,0},{8,4},{12,8},{16,12},{20,16},{24,20},{28,24},{0,28},{5,1},{9... | collective-permute-start | bytes 884744 | tf_op jit(solution)/shard_map/ppermute | solution.py:433
  27.2 10.4 %collective-permute-start = (f32[4,24,1024]{2,1,0:T(8,128)}, f32[4,24,1024]{2,1,0:T(8,128)S(1)}, u32[]{:S(2)}, u32[]{:S(2)}) collective-permute-start(f32[4,24,1024]{2,1,0:T(8,128)} %get-tuple-element.11.tail_ref), channel_id=1, source_target_pairs={{0,4},{4,8},{8,12},{12,16},{16,20},{20,24},{24,28},{28,0},{1,5},{5... | collective-permute-start | bytes 1179656 | tf_op jit(solution)/shard_map/ppermute | solution.py:432
  27.2 10.4 %copy-start = (f32[8,24,1024]{2,1,0:T(8,128)S(1)}, f32[8,24,1024]{2,1,0:T(8,128)}, u32[]{:S(2)}) copy-start(f32[8,24,1024]{2,1,0:T(8,128)} %get-tuple-element.10.mid_ref) | copy-start | bytes 2359300
  31.8 16.9 %all-to-all-start = ((f32[32,16,128]{2,1,0:T(8,128)}), f32[32,16,128]{2,1,0:T(8,128)S(1)}, u32[]{:S(2)}, u32[]{:S(2)}) async-start(f32[32,16,128]{2,1,0:T(8,128)} %shard_map.87), calls=%async_computation | async-start | bytes 524288 | tf_op jit(solution)/shard_map/all_to_all | solution.py:458
  37.8 11.9 %collective-permute-start.2 = (f32[8,4,1024]{2,1,0:T(4,128)S(1)}, f32[8,4,1024]{2,1,0:T(4,128)S(1)}, u32[]{:S(2)}, u32[]{:S(2)}) collective-permute-start(f32[8,4,1024]{2,1,0:T(4,128)S(1)} %get-tuple-element.18), channel_id=1, source_target_pairs={{0,1},{1,2},{2,3},{3,0},{4,5},{5,6},{6,7},{7,4},{8,9},{9,10},{10,1... | collective-permute-start | bytes 393224 | tf_op jit(solution)/shard_map/ppermute | solution.py:432
  39.6 10.1 %collective-permute-start.3 = (f32[8,4,1024]{2,1,0:T(4,128)S(1)}, f32[8,4,1024]{2,1,0:T(4,128)S(1)}, u32[]{:S(2)}, u32[]{:S(2)}) collective-permute-start(f32[8,4,1024]{2,1,0:T(4,128)S(1)} %get-tuple-element.19), channel_id=1, source_target_pairs={{1,0},{2,1},{3,2},{0,3},{5,4},{6,5},{7,6},{4,7},{9,8},{10,9},{11,1... | collective-permute-start | bytes 393224 | tf_op jit(solution)/shard_map/ppermute | solution.py:433

commit v5 on v4

--- a/solution.py
+++ b/solution.py
@@ -96,7 +96,7 @@
             now = times(now, step)
 
 
-def transforms(grid_ref, table_ref, phase_y_ref, phase_x_ref, along_z_ref, half_ref, wave_ref, out_ref, late):
+def transforms(grid_ref, table_ref, phase_y_ref, phase_x_ref, along_z_ref, half_ref, wave_ref, out_ref):
     rows_x, rows_y, depth = grid_ref.shape
     wide = wave_ref.shape[1]
 
@@ -106,8 +106,6 @@
     value, rest = split(grid_ref[...].reshape(rows_x * rows_y, depth))
     found = dot(value, table_ref[0]) + (dot(value, table_ref[1]) + dot(rest, table_ref[0]))
     along_z_ref[...] = found.reshape(rows_x, rows_y, 2 * wide)
-    for copy in late:
-        copy.wait()
     group = 5 if rows_x % 5 == 0 else 1
     for x in range(0, rows_x, group):
         real = [jnp.zeros((16, wide), jnp.float32)] * group
@@ -146,7 +144,7 @@
         out_ref[piece] = turned[16 * w : 16 * w + 16, part * lanes : (part + 1) * lanes]
 
 
-def deposit_column(column, fetches, next_fetches, cell_ref, frac_ref, weight_ref, count_ref, rows_ref, edge_ref, line_ref):
+def deposit_column(column, cell_ref, frac_ref, weight_ref, count_ref, rows_ref, edge_ref, line_ref):
     cap, blocks_z = weight_ref.shape
     depth = 8 * blocks_z
     half = blocks_z // 2
@@ -158,8 +156,6 @@
 
     line_ref[...] = jnp.zeros_like(line_ref)
     for d in range(3):
-        fetches[2 * d].wait()
-        fetches[2 * d + 1].wait()
         cell = cell_ref[d].astype(jnp.float32)
         place = cell + frac_ref[d]
         if d == 0:
@@ -170,10 +166,8 @@
         else:
             rows_ref[2 * d + 1] = paired(place * SCALE)
             rows_ref[2 * d + 2] = paired(cell)
-    fetches[6].wait()
     slots = lax.broadcasted_iota(jnp.int32, (cap, blocks_z), 0)
     rows_ref[7] = paired(jnp.where(slots < count_ref[0, pl.ds(column, 1), :], weight_ref[...], 0.0))
-    next_fetches()
     row = lax.broadcasted_iota(jnp.int32, (8, 128), 0)
     row8 = row.astype(jnp.float32)
     low = (row8 - 4.0) * SCALE
@@ -259,8 +253,8 @@
     lax.fori_loop(0, half // UNROLL, group, 0)
 
 
-def add_column(column, line_ref, grid_ref, finished):
-    depth = grid_ref.shape[2]
+def add_column(column, line_ref, faces):
+    depth = faces[0].shape[2]
     for n in range(4):
         line_ref[n, 4:8, :] += line_ref[n, depth + 4 : depth + 8, :]
         line_ref[n, depth : depth + 4, :] += line_ref[n, 0:4, :]
@@ -271,160 +265,107 @@
             for k in range(4):
                 near = k - 1.5
                 factor = NORMAL * math.exp((-near * (4 * n - 6) - 0.5 * near * near) / KERNEL_SIGMA**2)
-                grid_ref[4 * n + k, at, 128 * c : 128 * c + 128] += turned[16 * k : 16 * k + 16] * factor
-        finished(n)
-
-
-def deposit_body(
-    h_ref, k_ref, l_ref, count_ref, cell_ref, frac_ref, weight_ref,
-    head_ref, mid_ref, tail_ref, table_out_ref, phase_y_out_ref, phase_x_out_ref,
-    cells_ref, fracs_ref, weights_ref, rows_ref, edge_ref, line_ref, grid_ref, shift_ref,
-    table_ref, phase_y_ref, phase_x_ref, in_sems, out_sems, *, totals,
+                face = faces[(n + 1) // 2]
+                row = 4 * n + k - (1, 4, 12)[(n + 1) // 2]
+                if row >= 0:
+                    face[row, at, 128 * c : 128 * c + 128] += turned[16 * k : 16 * k + 16] * factor
+
+
+def deposit_body(count_ref, cell_ref, frac_ref, weight_ref, head_ref, mid_ref, tail_ref, rows_ref, edge_ref, line_ref):
+    column = pl.program_id(0)
+    faces = (head_ref, mid_ref, tail_ref)
+
+    @pl.when(column == 0)
+    def _():
+        for face in faces:
+            face[...] = jnp.zeros_like(face)
+
+    deposit_column(
+        column, cell_ref.at[:, 0, 0], frac_ref.at[:, 0, 0], weight_ref.at[0, 0], count_ref, rows_ref, edge_ref, line_ref
+    )
+    add_column(column, line_ref, faces)
+
+
+def transform_body(
+    h_ref, k_ref, l_ref, head_ref, mid_ref, tail_ref, out_ref, grid_ref, shift_ref,
+    table_ref, phase_y_ref, phase_x_ref, along_z_ref, half_ref, wave_ref, sems, *, totals,
 ):
-    columns = weights_ref.shape[0]
     rows_x, rows_y, depth = grid_ref.shape
-
-    def fetches(j):
-        found = []
-        for d in range(3):
-            found.append(pltpu.make_async_copy(cell_ref.at[d, 0, j], cells_ref.at[j, d], in_sems.at[j, 2 * d]))
-            found.append(pltpu.make_async_copy(frac_ref.at[d, 0, j], fracs_ref.at[j, d], in_sems.at[j, 2 * d + 1]))
-        found.append(pltpu.make_async_copy(weight_ref.at[0, j], weights_ref.at[j], in_sems.at[j, 6]))
-        return found
-
-    for copy in fetches(0):
-        copy.start()
-    place = (lax.axis_index("gx") * (rows_x - 8) - 3, lax.axis_index("gy") * (rows_y - 8) - 4)
+    copies = []
+    start = 0
+    for n, ref in enumerate((head_ref, mid_ref, tail_ref)):
+        copies.append(pltpu.make_async_copy(ref, grid_ref.at[pl.ds(start, ref.shape[0])], sems.at[n]))
+        copies[-1].start()
+        start += ref.shape[0]
+    place = (lax.axis_index("gx") * (rows_x - 7) - 3, lax.axis_index("gy") * (rows_y - 8) - 4)
     phase_tables(
         place, (h_ref, k_ref, l_ref), (*totals, depth), shift_ref, table_ref, phase_y_ref, phase_x_ref
     )
-    leaving = [
-        pltpu.make_async_copy(table_ref, table_out_ref, out_sems.at[0]),
-        pltpu.make_async_copy(phase_y_ref, phase_y_out_ref, out_sems.at[1]),
-        pltpu.make_async_copy(phase_x_ref, phase_x_out_ref, out_sems.at[2]),
-    ]
-    for copy in leaving:
-        copy.start()
-    grid_ref[...] = jnp.zeros_like(grid_ref)
-
-    def column(j, carry):
-        def next_fetches():
-            @pl.when(j < columns - 1)
-            def _():
-                for copy in fetches(j + 1):
-                    copy.start()
-
-        deposit_column(
-            j, fetches(j), next_fetches, cells_ref.at[j], fracs_ref.at[j], weights_ref.at[j], count_ref, rows_ref, edge_ref, line_ref
-        )
-
-        @pl.when(j < columns - 1)
-        def _():
-            add_column(j, line_ref, grid_ref, lambda n: None)
-
-        return carry
-
-    lax.fori_loop(0, columns, column, 0)
-
-    def finished(n):
-        if n != 1:
-            face, start = {0: (head_ref, 1), 2: (mid_ref, 4), 3: (tail_ref, 12)}[n]
-            copy = pltpu.make_async_copy(
-                grid_ref.at[pl.ds(start, face.shape[0])], face, out_sems.at[len(leaving)]
-            )
-            copy.start()
-            leaving.append(copy)
-
-    add_column(columns - 1, line_ref, grid_ref, finished)
-    for copy in leaving:
+    for copy in copies:
         copy.wait()
-
-
-def transform_body(
-    head_ref, mid_ref, tail_ref, table_in_ref, phase_y_in_ref, phase_x_in_ref, out_ref,
-    grid_ref, table_ref, phase_y_ref, phase_x_ref, along_z_ref, half_ref, wave_ref, sems,
-):
-    faces = []
-    start = 0
-    for n, ref in enumerate((head_ref, mid_ref, tail_ref)):
-        faces.append(pltpu.make_async_copy(ref, grid_ref.at[pl.ds(start, ref.shape[0])], sems.at[n]))
-        start += ref.shape[0]
-    tables = [
-        pltpu.make_async_copy(table_in_ref, table_ref, sems.at[3]),
-        pltpu.make_async_copy(phase_y_in_ref, phase_y_ref, sems.at[4]),
-        pltpu.make_async_copy(phase_x_in_ref, phase_x_ref, sems.at[5]),
-    ]
-    tables[0].start()
-    for copy in faces:
-        copy.start()
-    for copy in tables[1:]:
-        copy.start()
-    tables[0].wait()
-    for copy in faces:
-        copy.wait()
-    transforms(grid_ref, table_ref, phase_y_ref, phase_x_ref, along_z_ref, half_ref, wave_ref, out_ref, tables[1:])
+    transforms(grid_ref, table_ref, phase_y_ref, phase_x_ref, along_z_ref, half_ref, wave_ref, out_ref)
 
 
 FAR_AWAY = pl.BlockSpec(memory_space=pl.ANY)
 NEARBY = pl.BlockSpec(memory_space=pltpu.VMEM)
 
 
-def deposit(cell, frac, weight, count, miller_h, miller_k, miller_l, totals):
+def deposit(cell, frac, weight, count):
     _, columns, blocks_z, cap = weight.shape
     depth = 8 * blocks_z
-    rows_x, rows_y = 16, 8 * columns + 8
-    wide = 16 * miller_h.shape[0]
+    rows_y = 8 * columns + 8
 
     def turned(value):
         return jnp.swapaxes(value, -1, -2)
 
-    smem = pl.BlockSpec(memory_space=pltpu.SMEM)
     f32 = jnp.float32
-    tables = [((2, depth, 2 * wide), jnp.bfloat16), ((rows_y, 32, wide), f32), ((rows_x - 1, 32, wide), f32)]
+    faces = [(n, rows_y, depth) for n in (3, 8, 4)]
+    atoms = pl.BlockSpec((3, 1, 1, cap, blocks_z), lambda j: (0, 0, j, 0, 0))
     return pl.pallas_call(
-        functools.partial(deposit_body, totals=totals),
-        in_specs=[smem, smem, smem, NEARBY, FAR_AWAY, FAR_AWAY, FAR_AWAY],
-        out_specs=[FAR_AWAY] * 6,
-        out_shape=[jax.ShapeDtypeStruct((n, rows_y, depth), f32) for n in (3, 8, 4)]
-        + [jax.ShapeDtypeStruct(*table) for table in tables],
+        deposit_body,
+        grid=(columns,),
+        in_specs=[
+            pl.BlockSpec(count.shape, lambda j: (0, 0, 0)),
+            atoms,
+            atoms,
+            pl.BlockSpec((1, 1, cap, blocks_z), lambda j: (0, j, 0, 0)),
+        ],
+        out_specs=[pl.BlockSpec(face, lambda j: (0, 0, 0)) for face in faces],
+        out_shape=[jax.ShapeDtypeStruct(face, f32) for face in faces],
         scratch_shapes=[
-            pltpu.VMEM((columns, 3, cap, blocks_z), jnp.int32),
-            pltpu.VMEM((columns, 3, cap, blocks_z), f32),
-            pltpu.VMEM((columns, cap, blocks_z), f32),
             pltpu.VMEM((8, blocks_z // 2 // UNROLL, UNROLL, 2 * cap), f32),
             pltpu.VMEM((2 * (2 * cap // 128), 16, 128), f32),
             pltpu.VMEM((4, depth + 8, 64), f32),
-            pltpu.VMEM((rows_x, rows_y, depth), f32),
-            pltpu.VMEM((2, depth // FINE, wide), f32),
-            *[pltpu.VMEM(*table) for table in tables],
-            pltpu.SemaphoreType.DMA((columns, 7)),
-            pltpu.SemaphoreType.DMA((6,)),
         ],
-        compiler_params=pltpu.CompilerParams(vmem_limit_bytes=60 << 20),
-    )(miller_h, miller_k, miller_l, count, turned(cell), turned(frac), turned(weight))
-
-
-def transform(faces, tables, pieces):
+        compiler_params=pltpu.CompilerParams(vmem_limit_bytes=62 << 20),
+    )(count, turned(cell), turned(frac), turned(weight))
+
+
+def transform(faces, miller_h, miller_k, miller_l, totals, pieces):
     _, rows_y, depth = faces[0].shape
     rows_x = sum(face.shape[0] for face in faces)
-    wide = tables[1].shape[2]
+    wide = 16 * miller_h.shape[0]
+    smem = pl.BlockSpec(memory_space=pltpu.SMEM)
     f32 = jnp.float32
     return pl.pallas_call(
-        transform_body,
-        in_specs=[FAR_AWAY] * 6,
+        functools.partial(transform_body, totals=totals),
+        in_specs=[smem] * 3 + [FAR_AWAY] * 3,
         out_specs=NEARBY,
         out_shape=jax.ShapeDtypeStruct((pieces, 16, 32 * wide // pieces), f32),
         scratch_shapes=[
             pltpu.VMEM((rows_x, rows_y, depth), f32),
-            *[pltpu.VMEM(table.shape, table.dtype) for table in tables],
+            pltpu.VMEM((2, depth // FINE, wide), f32),
+            pltpu.VMEM((2, depth, 2 * wide), jnp.bfloat16),
+            pltpu.VMEM((rows_y, 32, wide), f32),
+            pltpu.VMEM((rows_x, 32, wide), f32),
             pltpu.VMEM((rows_x, rows_y, 2 * wide), f32),
             pltpu.VMEM((rows_x, 32, wide), f32),
             pltpu.VMEM((512, wide), f32),
-            pltpu.SemaphoreType.DMA((6,)),
+            pltpu.SemaphoreType.DMA((3,)),
         ],
-        compiler_params=pltpu.CompilerParams(vmem_limit_bytes=60 << 20),
+        compiler_params=pltpu.CompilerParams(vmem_limit_bytes=62 << 20),
         cost_estimate=pl.CostEstimate(flops=5_000_000_000, bytes_accessed=8_000_000, transcendentals=0),
-    )(*faces, *tables)
+    )(miller_h, miller_k, miller_l, *faces)
 
 
 def exchange(head, tail, axis):
@@ -449,11 +390,9 @@
     width_x, width_y, depth = 8 * blocks_x, 8 * blocks_y, 8 * blocks_z
     total_x, total_y = width_x * count_x, width_y * count_y
     pieces = count_x * count_y
-    head, mid, tail, *tables = deposit(
-        atom_cell, atom_frac, atom_weight, block_count, miller_h, miller_k, miller_l, (total_x, total_y)
-    )
+    head, mid, tail = deposit(atom_cell, atom_frac, atom_weight, block_count)
     before, after = exchange(head, tail, "gx")
-    waves = transform((head, mid, tail), tables, pieces)
+    waves = transform((head, mid, tail), miller_h, miller_k, miller_l, (total_x, total_y), pieces)
     before, after, _ = lax.optimization_barrier((before, after, waves))
     received = lax.all_to_all(waves, ("gx", "gy"), 0, 0, tiled=False)
     rows = miller_h.shape[0] * 16 // pieces

time: 50.8 us -> 50.1 us (0.986)
  Pallas kernels: 26.6 us -> 25.9 us
    pallas_call x2, Pallas kernels: 26.6 us -> 25.9 us  [the longest x1 21 us: deposit(): pl.pallas_call(deposit_body, grid=(columns,), in_specs=[pl.BlockSpec(coun...]
  transfers between devices with their start and end apart: 5 -> 5, of which waited for: 1 -> 1; matrix products, arithmetic and copies ran while one was open for 2% -> 2% of each run, Pallas kernels for 9% -> 10%
where the time goes in v5:
time: 50.1 us; the launch traced here: 49.8 us
  Pallas kernels  25.9 us (52%)
  starting transfers between devices  13.3 us (27%)
  waiting for transfers between devices  7.91 us (16%)
  other arithmetic  1.13 us (2%)
  local copies, waits for them, and re-layouts  0.94 us (2%)
  between operations  0.71 us (1%)
    pallas_call x1, Pallas kernels, deposit(): pl.pallas_call(deposit_body, grid=(columns,), in_specs=[pl.BlockSpec(coun...  21 us
    all_to_all x1, waiting for transfers between devices, shards(): received = lax.all_to_all(waves, ('gx', 'gy'), 0, 0, tiled=False)  7.9 us
    all_to_all x1, starting transfers between devices, shards(): received = lax.all_to_all(waves, ('gx', 'gy'), 0, 0, tiled=False)  5.8 us
    ppermute x2, starting transfers between devices, exchange(): lax.ppermute(head, axis, [((i + 1) % count, i) for i in range(count)])  5.64 us
    pallas_call x1, Pallas kernels, transform(): pl.pallas_call(functools.partial(transform_body, totals=totals), in_specs...  4.9 us
    ppermute x2, starting transfers between devices, exchange(): lax.ppermute(tail, axis, [(i, (i + 1) % count) for i in range(count)])  1.82 us
  transfers between devices with their start and end apart: 5, of which 1 were waited for; matrix products, arithmetic and copies ran while one was open for 2% of the time, Pallas kernels for 10%

profile of v5, /device:TPU:0, one launch (start us, length us, event | category | flops | bytes accessed | tf_op | source)
XLA Modules:
  0.0 49.8 jit_solution(10648168202369108014)
XLA Ops:
  0.6 21.0 %shard_map.86 = (f32[3,24,1024]{2,1,0:T(8,128)}, f32[8,24,1024]{2,1,0:T(8,128)}, f32[4,24,1024]{2,1,0:T(8,128)}) custom-call(s32[1,2,128]{2,1,0:T(2,128)} %count_ref.1, s32[3,1,2,576,128]{4,3,2,1,0:T(8,128)} %bitcast.5, f32[3,1,2,576,128]{4,3,2,1,0:T(8,128)} %bitcast.6, f32[1,2,576,128]{3,2,1,0:T(8,128)} %bitcast.7), custom_call_target="tpu_custom_call" | custom-call | tf_op jit(solution)/shard_map/pallas_call | solution.py:324
  21.6 4.5 %collective-permute-start.1 = (f32[3,24,1024]{2,1,0:T(8,128)}, f32[3,24,1024]{2,1,0:T(8,128)S(1)}, u32[]{:S(2)}, u32[]{:S(2)}) collective-permute-start(f32[3,24,1024]{2,1,0:T(8,128)} %get-tuple-element.9.head_ref), channel_id=1, source_target_pairs={{4,0},{8,4},{12,8},{16,12},{20,16},{24,20},{28,24},{0,28},{5,1},{9... | collective-permute-start | bytes 884744 | tf_op jit(solution)/shard_map/ppermute | solution.py:374
  26.1 0.0 collective-permute-start
  26.1 0.0 copy-start
  26.1 4.9 %shard_map.87 = f32[32,16,128]{2,1,0:T(8,128)} custom-call(s32[8]{0:T(128)} %h_ref.1, s32[8]{0:T(128)} %k_ref.1, s32[8]{0:T(128)} %l_ref.1, f32[3,24,1024]{2,1,0:T(8,128)} %get-tuple-element.9.head_ref, f32[8,24,1024]{2,1,0:T(8,128)} %get-tuple-element.7.mid_ref, f32[4,24,1024]{2,1,0:T(8,128)} %get-tuple-element.8.tail_ref), custom_call_target="tpu_custom_call" | custom-call | flops 5000000000 | bytes 8000000 | tf_op jit(solution)/shard_map/pallas_call | solution.py:350
  31.0 5.8 %all-to-all-start = ((f32[32,16,128]{2,1,0:T(8,128)}), f32[32,16,128]{2,1,0:T(8,128)S(1)}, u32[]{:S(2)}, u32[]{:S(2)}) async-start(f32[32,16,128]{2,1,0:T(8,128)} %shard_map.87), calls=%async_computation | async-start | bytes 524288 | tf_op jit(solution)/shard_map/all_to_all | solution.py:397
  36.8 0.0 collective-permute-done.1
  36.8 0.0 collective-permute-done
  36.8 0.0 copy-done
  36.8 0.1 pad_add_fusion
  36.9 0.1 fusion.2
  37.0 1.8 %collective-permute-start.2 = (f32[8,4,1024]{2,1,0:T(4,128)S(1)}, f32[8,4,1024]{2,1,0:T(4,128)S(1)}, u32[]{:S(2)}, u32[]{:S(2)}) collective-permute-start(f32[8,4,1024]{2,1,0:T(4,128)S(1)} %get-tuple-element.12), channel_id=1, source_target_pairs={{0,1},{1,2},{2,3},{3,0},{4,5},{5,6},{6,7},{7,4},{8,9},{9,10},{10,1... | collective-permute-start | bytes 393224 | tf_op jit(solution)/shard_map/ppermute | solution.py:373
  38.8 1.2 %collective-permute-start.3 = (f32[8,4,1024]{2,1,0:T(4,128)S(1)}, f32[8,4,1024]{2,1,0:T(4,128)S(1)}, u32[]{:S(2)}, u32[]{:S(2)}) collective-permute-start(f32[8,4,1024]{2,1,0:T(4,128)S(1)} %get-tuple-element.13), channel_id=1, source_target_pairs={{1,0},{2,1},{3,2},{0,3},{5,4},{6,5},{7,6},{4,7},{9,8},{10,9},{11,1... | collective-permute-start | bytes 393224 | tf_op jit(solution)/shard_map/ppermute | solution.py:374
  40.0 7.9 %all-to-all-done = f32[32,16,128]{2,1,0:T(8,128)S(1)} async-done(((f32[32,16,128]{2,1,0:T(8,128)}), f32[32,16,128]{2,1,0:T(8,128)S(1)}, u32[]{:S(2)}, u32[]{:S(2)}) %all-to-all-start) | async-done | bytes 262176 | tf_op jit(solution)/shard_map/all_to_all | solution.py:397
  47.9 0.1 mul.7
  48.0 0.1 reduce_sum.19
  48.2 0.1 copy.10
  48.2 0.7 %reshape.9 = f32[4,256]{1,0:T(4,128)} reshape(f32[4,16,16]{2,1,0:T(8,128)S(1)} %copy.10) | data formatting | bytes 8192 | tf_op jit(solution)/shard_map/reshape | solution.py:401
  48.9 0.0 collective-permute-done.2
  48.9 0.0 collective-permute-done.3
  48.9 0.9 %fusion = f32[8,16,1024]{2,1,0:T(8,128)} fusion(f32[8,24,1024]{2,1,0:T(8,128)S(1)} %pad_add_fusion, f32[8,4,1024]{2,1,0:T(4,128)S(1)} %collective-permute-done.3, f32[8,4,1024]{2,1,0:T(4,128)S(1)} %collective-permute-done.2), kind=kLoop, calls=%fused_computation.2 | loop fusion | flops 262144 | bytes 1310720 | tf_op jit(solution)/shard_map/add | solution.py:384
  (3 shorter events, 0.0 us)
Async XLA Ops:
  21.6 15.2 %collective-permute-start.1 = (f32[3,24,1024]{2,1,0:T(8,128)}, f32[3,24,1024]{2,1,0:T(8,128)S(1)}, u32[]{:S(2)}, u32[]{:S(2)}) collective-permute-start(f32[3,24,1024]{2,1,0:T(8,128)} %get-tuple-element.9.head_ref), channel_id=1, source_target_pairs={{4,0},{8,4},{12,8},{16,12},{20,16},{24,20},{28,24},{0,28},{5,1},{9... | collective-permute-start | bytes 884744 | tf_op jit(solution)/shard_map/ppermute | solution.py:374
  26.1 10.7 %collective-permute-start = (f32[4,24,1024]{2,1,0:T(8,128)}, f32[4,24,1024]{2,1,0:T(8,128)S(1)}, u32[]{:S(2)}, u32[]{:S(2)}) collective-permute-start(f32[4,24,1024]{2,1,0:T(8,128)} %get-tuple-element.8.tail_ref), channel_id=1, source_target_pairs={{0,4},{4,8},{8,12},{12,16},{16,20},{20,24},{24,28},{28,0},{1,5},{5... | collective-permute-start | bytes 1179656 | tf_op jit(solution)/shard_map/ppermute | solution.py:373
  26.1 10.7 %copy-start = (f32[8,24,1024]{2,1,0:T(8,128)S(1)}, f32[8,24,1024]{2,1,0:T(8,128)}, u32[]{:S(2)}) copy-start(f32[8,24,1024]{2,1,0:T(8,128)} %get-tuple-element.7.mid_ref) | copy-start | bytes 2359300
  31.0 16.9 %all-to-all-start = ((f32[32,16,128]{2,1,0:T(8,128)}), f32[32,16,128]{2,1,0:T(8,128)S(1)}, u32[]{:S(2)}, u32[]{:S(2)}) async-start(f32[32,16,128]{2,1,0:T(8,128)} %shard_map.87), calls=%async_computation | async-start | bytes 524288 | tf_op jit(solution)/shard_map/all_to_all | solution.py:397
  37.0 11.9 %collective-permute-start.2 = (f32[8,4,1024]{2,1,0:T(4,128)S(1)}, f32[8,4,1024]{2,1,0:T(4,128)S(1)}, u32[]{:S(2)}, u32[]{:S(2)}) collective-permute-start(f32[8,4,1024]{2,1,0:T(4,128)S(1)} %get-tuple-element.12), channel_id=1, source_target_pairs={{0,1},{1,2},{2,3},{3,0},{4,5},{5,6},{6,7},{7,4},{8,9},{9,10},{10,1... | collective-permute-start | bytes 393224 | tf_op jit(solution)/shard_map/ppermute | solution.py:373
  38.8 10.1 %collective-permute-start.3 = (f32[8,4,1024]{2,1,0:T(4,128)S(1)}, f32[8,4,1024]{2,1,0:T(4,128)S(1)}, u32[]{:S(2)}, u32[]{:S(2)}) collective-permute-start(f32[8,4,1024]{2,1,0:T(4,128)S(1)} %get-tuple-element.13), channel_id=1, source_target_pairs={{1,0},{2,1},{3,2},{0,3},{5,4},{6,5},{7,6},{4,7},{9,8},{10,9},{11,1... | collective-permute-start | bytes 393224 | tf_op jit(solution)/shard_map/ppermute | solution.py:374

commit v6 on v5

--- a/solution.py
+++ b/solution.py
@@ -96,14 +96,16 @@
             now = times(now, step)
 
 
-def transforms(grid_ref, table_ref, phase_y_ref, phase_x_ref, along_z_ref, half_ref, wave_ref, out_ref):
-    rows_x, rows_y, depth = grid_ref.shape
+def transforms(faces, table_ref, phase_y_ref, phase_x_ref, along_z_ref, half_ref, wave_ref, out_ref):
+    rows_x, rows_y, _ = along_z_ref.shape
+    depth = faces[0].shape[2]
     wide = wave_ref.shape[1]
 
     def dot(a, b):
         return jnp.dot(a, b, preferred_element_type=jnp.float32)
 
-    value, rest = split(grid_ref[...].reshape(rows_x * rows_y, depth))
+    grid = jnp.concatenate([face[...].reshape(face.shape[0] * rows_y, depth) for face in faces], axis=0)
+    value, rest = split(grid)
     found = dot(value, table_ref[0]) + (dot(value, table_ref[1]) + dot(rest, table_ref[0]))
     along_z_ref[...] = found.reshape(rows_x, rows_y, 2 * wide)
     group = 5 if rows_x % 5 == 0 else 1
@@ -271,12 +273,22 @@
                     face[row, at, 128 * c : 128 * c + 128] += turned[16 * k : 16 * k + 16] * factor
 
 
-def deposit_body(count_ref, cell_ref, frac_ref, weight_ref, head_ref, mid_ref, tail_ref, rows_ref, edge_ref, line_ref):
+def whole_body(
+    h_ref, k_ref, l_ref, count_ref, cell_ref, frac_ref, weight_ref, head_ref, mid_ref, tail_ref, out_ref,
+    rows_ref, edge_ref, line_ref, shift_ref, table_ref, phase_y_ref, phase_x_ref, along_z_ref, half_ref, wave_ref,
+    *, totals,
+):
     column = pl.program_id(0)
     faces = (head_ref, mid_ref, tail_ref)
+    rows_x, rows_y, _ = along_z_ref.shape
+    depth = mid_ref.shape[2]
 
     @pl.when(column == 0)
     def _():
+        place = (lax.axis_index("gx") * (rows_x - 7) - 3, lax.axis_index("gy") * (rows_y - 8) - 4)
+        phase_tables(
+            place, (h_ref, k_ref, l_ref), (*totals, depth), shift_ref, table_ref, phase_y_ref, phase_x_ref
+        )
         for face in faces:
             face[...] = jnp.zeros_like(face)
 
@@ -285,75 +297,42 @@
     )
     add_column(column, line_ref, faces)
 
-
-def transform_body(
-    h_ref, k_ref, l_ref, head_ref, mid_ref, tail_ref, out_ref, grid_ref, shift_ref,
-    table_ref, phase_y_ref, phase_x_ref, along_z_ref, half_ref, wave_ref, sems, *, totals,
-):
-    rows_x, rows_y, depth = grid_ref.shape
-    copies = []
-    start = 0
-    for n, ref in enumerate((head_ref, mid_ref, tail_ref)):
-        copies.append(pltpu.make_async_copy(ref, grid_ref.at[pl.ds(start, ref.shape[0])], sems.at[n]))
-        copies[-1].start()
-        start += ref.shape[0]
-    place = (lax.axis_index("gx") * (rows_x - 7) - 3, lax.axis_index("gy") * (rows_y - 8) - 4)
-    phase_tables(
-        place, (h_ref, k_ref, l_ref), (*totals, depth), shift_ref, table_ref, phase_y_ref, phase_x_ref
-    )
-    for copy in copies:
-        copy.wait()
-    transforms(grid_ref, table_ref, phase_y_ref, phase_x_ref, along_z_ref, half_ref, wave_ref, out_ref)
-
-
-FAR_AWAY = pl.BlockSpec(memory_space=pl.ANY)
-NEARBY = pl.BlockSpec(memory_space=pltpu.VMEM)
-
-
-def deposit(cell, frac, weight, count):
+    @pl.when(column == pl.num_programs(0) - 1)
+    def _():
+        transforms(faces, table_ref, phase_y_ref, phase_x_ref, along_z_ref, half_ref, wave_ref, out_ref)
+
+
+def deposit_and_transform(cell, frac, weight, count, miller_h, miller_k, miller_l, totals, pieces):
     _, columns, blocks_z, cap = weight.shape
     depth = 8 * blocks_z
-    rows_y = 8 * columns + 8
+    rows_x, rows_y = 15, 8 * columns + 8
+    wide = 16 * miller_h.shape[0]
 
     def turned(value):
         return jnp.swapaxes(value, -1, -2)
 
     f32 = jnp.float32
-    faces = [(n, rows_y, depth) for n in (3, 8, 4)]
+    outs = [(n, rows_y, depth) for n in (3, 8, 4)] + [(pieces, 16, 32 * wide // pieces)]
     atoms = pl.BlockSpec((3, 1, 1, cap, blocks_z), lambda j: (0, 0, j, 0, 0))
+    smem = pl.BlockSpec(memory_space=pltpu.SMEM)
     return pl.pallas_call(
-        deposit_body,
+        functools.partial(whole_body, totals=totals),
         grid=(columns,),
         in_specs=[
+            smem,
+            smem,
+            smem,
             pl.BlockSpec(count.shape, lambda j: (0, 0, 0)),
             atoms,
             atoms,
             pl.BlockSpec((1, 1, cap, blocks_z), lambda j: (0, j, 0, 0)),
         ],
-        out_specs=[pl.BlockSpec(face, lambda j: (0, 0, 0)) for face in faces],
-        out_shape=[jax.ShapeDtypeStruct(face, f32) for face in faces],
+        out_specs=[pl.BlockSpec(out, lambda j: (0, 0, 0)) for out in outs],
+        out_shape=[jax.ShapeDtypeStruct(out, f32) for out in outs],
         scratch_shapes=[
             pltpu.VMEM((8, blocks_z // 2 // UNROLL, UNROLL, 2 * cap), f32),
             pltpu.VMEM((2 * (2 * cap // 128), 16, 128), f32),
             pltpu.VMEM((4, depth + 8, 64), f32),
-        ],
-        compiler_params=pltpu.CompilerParams(vmem_limit_bytes=62 << 20),
-    )(count, turned(cell), turned(frac), turned(weight))
-
-
-def transform(faces, miller_h, miller_k, miller_l, totals, pieces):
-    _, rows_y, depth = faces[0].shape
-    rows_x = sum(face.shape[0] for face in faces)
-    wide = 16 * miller_h.shape[0]
-    smem = pl.BlockSpec(memory_space=pltpu.SMEM)
-    f32 = jnp.float32
-    return pl.pallas_call(
-        functools.partial(transform_body, totals=totals),
-        in_specs=[smem] * 3 + [FAR_AWAY] * 3,
-        out_specs=NEARBY,
-        out_shape=jax.ShapeDtypeStruct((pieces, 16, 32 * wide // pieces), f32),
-        scratch_shapes=[
-            pltpu.VMEM((rows_x, rows_y, depth), f32),
             pltpu.VMEM((2, depth // FINE, wide), f32),
             pltpu.VMEM((2, depth, 2 * wide), jnp.bfloat16),
             pltpu.VMEM((rows_y, 32, wide), f32),
@@ -361,11 +340,9 @@
             pltpu.VMEM((rows_x, rows_y, 2 * wide), f32),
             pltpu.VMEM((rows_x, 32, wide), f32),
             pltpu.VMEM((512, wide), f32),
-            pltpu.SemaphoreType.DMA((3,)),
         ],
         compiler_params=pltpu.CompilerParams(vmem_limit_bytes=62 << 20),
-        cost_estimate=pl.CostEstimate(flops=5_000_000_000, bytes_accessed=8_000_000, transcendentals=0),
-    )(miller_h, miller_k, miller_l, *faces)
+    )(miller_h, miller_k, miller_l, count, turned(cell), turned(frac), turned(weight))
 
 
 def exchange(head, tail, axis):
@@ -390,11 +367,11 @@
     width_x, width_y, depth = 8 * blocks_x, 8 * blocks_y, 8 * blocks_z
     total_x, total_y = width_x * count_x, width_y * count_y
     pieces = count_x * count_y
-    head, mid, tail = deposit(atom_cell, atom_frac, atom_weight, block_count)
+    head, mid, tail, waves = deposit_and_transform(
+        atom_cell, atom_frac, atom_weight, block_count, miller_h, miller_k, miller_l, (total_x, total_y), pieces
+    )
+    received = lax.all_to_all(waves, ("gx", "gy"), 0, 0, tiled=False)
     before, after = exchange(head, tail, "gx")
-    waves = transform((head, mid, tail), miller_h, miller_k, miller_l, (total_x, total_y), pieces)
-    before, after, _ = lax.optimization_barrier((before, after, waves))
-    received = lax.all_to_all(waves, ("gx", "gy"), 0, 0, tiled=False)
     rows = miller_h.shape[0] * 16 // pieces
     summed = jnp.sum(received, axis=0).reshape(16, rows, 2, 16)
     power = jnp.sum(summed * summed, axis=2) / float(total_x * total_y * depth)

time: 50.1 us -> 49.6 us (0.990)
  the two profiles are of different devices: /device:TPU:0 before, /device:TPU:1 now
where the time goes in v6:
time: 49.6 us; the launch traced here: 49.4 us
  Pallas kernels  23.9 us (48%)
  starting transfers between devices  11.6 us (23%)
  waiting for transfers between devices  9.97 us (20%)
  other arithmetic  2.26 us (5%)
  local copies, waits for them, and re-layouts  0.94 us (2%)
  between operations  0.68 us (1%)
    pallas_call x1, Pallas kernels, deposit_and_transform(): pl.pallas_call(functools.partial(whole_body, totals=totals), grid=(column...  23.9 us
    ppermute x2, waiting for transfers between devices, exchange(): lax.ppermute(head, axis, [((i + 1) % count, i) for i in range(count)])  7 us
    all_to_all x1, starting transfers between devices, shards(): received = lax.all_to_all(waves, ('gx', 'gy'), 0, 0, tiled=False)  6.15 us
    ppermute x2, starting transfers between devices, exchange(): lax.ppermute(tail, axis, [(i, (i + 1) % count) for i in range(count)])  4.44 us
    add x2, other arithmetic, added(): return inner + leading + jnp.pad(after, widths)  2.12 us
    ppermute x2, waiting for transfers between devices, exchange(): lax.ppermute(tail, axis, [(i, (i + 1) % count) for i in range(count)])  1.73 us
    all_to_all x1, waiting for transfers between devices, shards(): received = lax.all_to_all(waves, ('gx', 'gy'), 0, 0, tiled=False)  1.23 us
    ppermute x2, starting transfers between devices, exchange(): lax.ppermute(head, axis, [((i + 1) % count, i) for i in range(count)])  1.04 us
  transfers between devices with their start and end apart: 5, of which 4 were waited for; matrix products, arithmetic and copies ran while one was open for 5% of the time, Pallas kernels for 0%

profile of v6, /device:TPU:1, one launch (start us, length us, event | category | flops | bytes accessed | tf_op | source)
XLA Modules:
  0.0 49.4 jit_solution(13496652560140756031)
XLA Ops:
  0.6 23.9 %shard_map.86 = (f32[3,24,1024]{2,1,0:T(8,128)}, f32[8,24,1024]{2,1,0:T(8,128)}, f32[4,24,1024]{2,1,0:T(8,128)}, f32[32,16,128]{2,1,0:T(8,128)}) custom-call(s32[8]{0:T(128)} %h_ref.1, s32[8]{0:T(128)} %k_ref.1, s32[8]{0:T(128)} %l_ref.1, s32[1,2,128]{2,1,0:T(2,128)} %count_ref.1, s32[3,1,2,576,128]{4,3,2,1,0:T(8,128)} %bitcast.5, ...), custom_call_target="tpu_custom_call" | custom-call | tf_op jit(solution)/shard_map/pallas_call | solution.py:318
  24.6 2.7 %collective-permute-start = (f32[4,24,1024]{2,1,0:T(8,128)}, f32[4,24,1024]{2,1,0:T(8,128)S(1)}, u32[]{:S(2)}, u32[]{:S(2)}) collective-permute-start(f32[4,24,1024]{2,1,0:T(8,128)} %get-tuple-element.7), channel_id=1, source_target_pairs={{0,4},{4,8},{8,12},{12,16},{16,20},{20,24},{24,28},{28,0},{1,5},{5... | collective-permute-start | bytes 1179656 | tf_op jit(solution)/shard_map/ppermute | solution.py:350
  27.3 0.0 collective-permute-start.1
  27.3 6.2 %all-to-all-start = ((f32[32,16,128]{2,1,0:T(8,128)}), f32[32,16,128]{2,1,0:T(8,128)S(1)}, u32[]{:S(2)}, u32[]{:S(2)}) async-start(f32[32,16,128]{2,1,0:T(8,128)} %get-tuple-element.9), calls=%async_computation | async-start | bytes 524288 | tf_op jit(solution)/shard_map/all_to_all | solution.py:373
  33.4 5.7 %collective-permute-done.1 = f32[3,24,1024]{2,1,0:T(8,128)S(1)} collective-permute-done((f32[3,24,1024]{2,1,0:T(8,128)}, f32[3,24,1024]{2,1,0:T(8,128)S(1)}, u32[]{:S(2)}, u32[]{:S(2)}) %collective-permute-start.1) | collective-permute-done | bytes 294944 | tf_op jit(solution)/shard_map/ppermute | solution.py:351
  39.1 0.0 collective-permute-done
  39.1 1.2 %pad_add_fusion = f32[8,24,1024]{2,1,0:T(8,128)S(1)} fusion(f32[3,24,1024]{2,1,0:T(8,128)S(1)} %collective-permute-done.1, f32[8,24,1024]{2,1,0:T(8,128)} %get-tuple-element.6, f32[4,24,1024]{2,1,0:T(8,128)S(1)} %collective-permute-done), kind=kLoop, calls=%fused_computation | loop fusion | flops 393216 | bytes 2260992 | tf_op jit(solution)/shard_map/add | solution.py:361
  40.3 0.1 fusion.2
  40.4 1.7 %collective-permute-start.2 = (f32[8,4,1024]{2,1,0:T(4,128)S(1)}, f32[8,4,1024]{2,1,0:T(4,128)S(1)}, u32[]{:S(2)}, u32[]{:S(2)}) collective-permute-start(f32[8,4,1024]{2,1,0:T(4,128)S(1)} %get-tuple-element.10), channel_id=1, source_target_pairs={{0,1},{1,2},{2,3},{3,0},{4,5},{5,6},{6,7},{7,4},{8,9},{9,10},{10,1... | collective-permute-start | bytes 393224 | tf_op jit(solution)/shard_map/ppermute | solution.py:350
  42.1 1.0 %collective-permute-start.3 = (f32[8,4,1024]{2,1,0:T(4,128)S(1)}, f32[8,4,1024]{2,1,0:T(4,128)S(1)}, u32[]{:S(2)}, u32[]{:S(2)}) collective-permute-start(f32[8,4,1024]{2,1,0:T(4,128)S(1)} %get-tuple-element.11), channel_id=1, source_target_pairs={{1,0},{2,1},{3,2},{0,3},{5,4},{6,5},{7,6},{4,7},{9,8},{10,9},{11,1... | collective-permute-start | bytes 393224 | tf_op jit(solution)/shard_map/ppermute | solution.py:351
  43.1 1.2 %all-to-all-done = f32[32,16,128]{2,1,0:T(8,128)S(1)} async-done(((f32[32,16,128]{2,1,0:T(8,128)}), f32[32,16,128]{2,1,0:T(8,128)S(1)}, u32[]{:S(2)}, u32[]{:S(2)}) %all-to-all-start) | async-done | bytes 262176 | tf_op jit(solution)/shard_map/all_to_all | solution.py:373
  44.4 0.1 mul.7
  44.6 0.1 reduce_sum.19
  44.7 0.1 copy.10
  44.7 0.7 %reshape.9 = f32[4,256]{1,0:T(4,128)} reshape(f32[4,16,16]{2,1,0:T(8,128)S(1)} %copy.10) | data formatting | bytes 8192 | tf_op jit(solution)/shard_map/reshape | solution.py:378
  45.4 1.7 %collective-permute-done.2 = f32[8,4,1024]{2,1,0:T(4,128)S(1)} collective-permute-done((f32[8,4,1024]{2,1,0:T(4,128)S(1)}, f32[8,4,1024]{2,1,0:T(4,128)S(1)}, u32[]{:S(2)}, u32[]{:S(2)}) %collective-permute-start.2) | collective-permute-done | bytes 131104 | tf_op jit(solution)/shard_map/ppermute | solution.py:350
  47.2 1.3 %collective-permute-done.3 = f32[8,4,1024]{2,1,0:T(4,128)S(1)} collective-permute-done((f32[8,4,1024]{2,1,0:T(4,128)S(1)}, f32[8,4,1024]{2,1,0:T(4,128)S(1)}, u32[]{:S(2)}, u32[]{:S(2)}) %collective-permute-start.3) | collective-permute-done | bytes 131104 | tf_op jit(solution)/shard_map/ppermute | solution.py:351
  48.5 0.9 %fusion = f32[8,16,1024]{2,1,0:T(8,128)} fusion(f32[8,24,1024]{2,1,0:T(8,128)S(1)} %pad_add_fusion, f32[8,4,1024]{2,1,0:T(4,128)S(1)} %collective-permute-done.3, f32[8,4,1024]{2,1,0:T(4,128)S(1)} %collective-permute-done.2), kind=kLoop, calls=%fused_computation.2 | loop fusion | flops 262144 | bytes 1310720 | tf_op jit(solution)/shard_map/add | solution.py:361
  (3 shorter events, 0.0 us)
Async XLA Ops:
  24.6 14.5 %collective-permute-start = (f32[4,24,1024]{2,1,0:T(8,128)}, f32[4,24,1024]{2,1,0:T(8,128)S(1)}, u32[]{:S(2)}, u32[]{:S(2)}) collective-permute-start(f32[4,24,1024]{2,1,0:T(8,128)} %get-tuple-element.7), channel_id=1, source_target_pairs={{0,4},{4,8},{8,12},{12,16},{16,20},{20,24},{24,28},{28,0},{1,5},{5... | collective-permute-start | bytes 1179656 | tf_op jit(solution)/shard_map/ppermute | solution.py:350
  27.3 11.8 %collective-permute-start.1 = (f32[3,24,1024]{2,1,0:T(8,128)}, f32[3,24,1024]{2,1,0:T(8,128)S(1)}, u32[]{:S(2)}, u32[]{:S(2)}) collective-permute-start(f32[3,24,1024]{2,1,0:T(8,128)} %get-tuple-element.8), channel_id=1, source_target_pairs={{4,0},{8,4},{12,8},{16,12},{20,16},{24,20},{28,24},{0,28},{5,1},{9... | collective-permute-start | bytes 884744 | tf_op jit(solution)/shard_map/ppermute | solution.py:351
  27.3 17.1 %all-to-all-start = ((f32[32,16,128]{2,1,0:T(8,128)}), f32[32,16,128]{2,1,0:T(8,128)S(1)}, u32[]{:S(2)}, u32[]{:S(2)}) async-start(f32[32,16,128]{2,1,0:T(8,128)} %get-tuple-element.9), calls=%async_computation | async-start | bytes 524288 | tf_op jit(solution)/shard_map/all_to_all | solution.py:373
  40.4 6.8 %collective-permute-start.2 = (f32[8,4,1024]{2,1,0:T(4,128)S(1)}, f32[8,4,1024]{2,1,0:T(4,128)S(1)}, u32[]{:S(2)}, u32[]{:S(2)}) collective-permute-start(f32[8,4,1024]{2,1,0:T(4,128)S(1)} %get-tuple-element.10), channel_id=1, source_target_pairs={{0,1},{1,2},{2,3},{3,0},{4,5},{5,6},{6,7},{7,4},{8,9},{9,10},{10,1... | collective-permute-start | bytes 393224 | tf_op jit(solution)/shard_map/ppermute | solution.py:350
  42.1 6.4 %collective-permute-start.3 = (f32[8,4,1024]{2,1,0:T(4,128)S(1)}, f32[8,4,1024]{2,1,0:T(4,128)S(1)}, u32[]{:S(2)}, u32[]{:S(2)}) collective-permute-start(f32[8,4,1024]{2,1,0:T(4,128)S(1)} %get-tuple-element.11), channel_id=1, source_target_pairs={{1,0},{2,1},{3,2},{0,3},{5,4},{6,5},{7,6},{4,7},{9,8},{10,9},{11,1... | collective-permute-start | bytes 393224 | tf_op jit(solution)/shard_map/ppermute | solution.py:351
